TPU v7x, 32 devices: a whole 2x2x4 slice. The times are simulated.
32 devices in a mesh: path: 16 (over z, y, core), fsdp: 2 (over x).
Axes of the slice: x: 2, y: 2, z: 4, core: 2. Of those that a mesh axis runs over, the one named last changes fastest.
Arguments:
- inputs: bfloat16 [16, 1536, 2048], P('path', 'fsdp'), may hold values from -6 to 6
- targets: bfloat16 [16, 1536, 2048], P('path', 'fsdp'), may hold values from -6 to 6
- token_ids: int32 [16, 1536], P('path', 'fsdp'), may hold values from 0 to 31999, as said below
- path_weights: bfloat16 [16, 2048, 2048], P('path', 'fsdp'), may hold values from -6 to 6
- stale_deltas: bfloat16 [16, 2048, 2048], P('path', 'fsdp'), may hold values from -6 to 6
- module_params: float32 [4, 2048, 2048], P(None, 'fsdp', 'path'), may hold values from -6 to 6
- momentum: float32 [4, 2048, 2048], P(None, 'fsdp', 'path'), may hold values from -3 to 3
- module_of_path: int32 [16], replicated, may hold values from 0 to 3, as said below
- sharing_counts: int32 [4], replicated, may hold values from 1 to 8, as said below
Outputs:
- next_weights: bfloat16 [16, 2048, 2048], P('path', 'fsdp')
- new_params: float32 [4, 2048, 2048], P(None, 'fsdp', 'path')
- new_momentum: float32 [4, 2048, 2048], P(None, 'fsdp', 'path')
Inputs may be any that keep to these rules, and one draw needn't show every extreme that they name: `module_of_path`: every module is used by at least one path; one module is used by exactly 8 paths, every other by fewer. sharing_counts[m] is the number of paths p with module_of_path[p] = m. `token_ids`: each path's tokens with id 0 form a suffix that leaves at least a quarter of its 1536 tokens real.
All inputs are finite; a program needn't handle non-finite values.
Results may differ from a plain program's by a relative error of at most 0.015.
Values may be sent and summed in bfloat16 or wider, within the bound.
A program may use at most 128 MiB of HBM per device.

v0:
```python
import math

import jax
import jax.numpy as jnp
from jax import lax
from jax.sharding import PartitionSpec as P


def per_device(
    inputs,
    targets,
    token_ids,
    path_weights,
    stale_deltas,
    module_params,
    momentum,
    module_of_path,
    sharing_counts,
):
    block_in = inputs[0]
    width_in = block_in.shape[-1]
    values = block_in.astype(jnp.float32)
    scale = lax.rsqrt(jnp.mean(values * values, axis=-1, keepdims=True) + 1e-06)
    normed = (values * scale).astype(jnp.bfloat16)
    mask = (token_ids[0] != 0).astype(jnp.float32)
    count = lax.psum(jnp.sum(mask), "fsdp")
    weights = path_weights[0]
    columns = normed
    projected = jnp.dot(
        columns,
        lax.all_gather(weights, "fsdp", axis=0, tiled=True),
        preferred_element_type=jnp.float32,
    ) / math.sqrt(width_in)
    residual_rows = ((projected - targets[0].astype(jnp.float32)) * mask[:, None]).astype(
        jnp.bfloat16
    )
    columns = normed
    grad = lax.psum_scatter(
        jnp.einsum("ti,tj->ij", columns, residual_rows, preferred_element_type=jnp.float32).astype(
            jnp.bfloat16
        ),
        "fsdp",
        scatter_dimension=0,
        tiled=True,
    ).astype(jnp.float32) / jnp.sqrt(count)
    inner = weights.astype(jnp.float32) - 0.25 * grad
    modules = sharing_counts.shape[0]
    labels = jnp.arange(modules, dtype=jnp.int32)
    mine = module_of_path[lax.axis_index("path")]
    mine_hot = (labels == mine).astype(jnp.float32)
    delta = stale_deltas[0]
    placed = mine_hot[:, None, None] * delta.astype(jnp.float32)[None]
    total = lax.psum_scatter(
        placed.astype(jnp.bfloat16), "path", scatter_dimension=2, tiled=True
    ).astype(jnp.float32)
    outer_grad = total / sharing_counts.astype(jnp.float32)[:, None, None]
    new_momentum = 0.9 * momentum + outer_grad
    outer_step = 0.7 * (outer_grad + 0.9 * new_momentum)
    new_params = module_params - outer_step
    outer_step_b = outer_step.astype(jnp.bfloat16)
    every_step = lax.all_gather(outer_step_b, "path", axis=2, tiled=True)
    correction = jnp.einsum(
        "m,mrc->rc", mine_hot.astype(jnp.bfloat16), every_step, preferred_element_type=jnp.float32
    )
    next_weights = (inner - correction).astype(jnp.bfloat16)[None]
    return (next_weights, new_params, new_momentum)


def solution(mesh):
    return jax.shard_map(
        per_device,
        mesh=mesh,
        in_specs=(
            P("path", "fsdp", None),
            P("path", "fsdp", None),
            P("path", "fsdp"),
            P("path", "fsdp", None),
            P("path", "fsdp", None),
            P(None, "fsdp", "path"),
            P(None, "fsdp", "path"),
            P(),
            P(),
        ),
        out_specs=(P("path", "fsdp", None), P(None, "fsdp", "path"), P(None, "fsdp", "path")),
        check_vma=False,
    )
```

profile of v0, /device:TPU:0, one launch (start us, length us, event | category | flops | bytes accessed | tf_op | source)
XLA Modules:
  0.0 500.8 jit_solution(12890503767215928950)
XLA Ops:
  8.0 0.0 reduce-scatter.7.cloned.1.call-start
  8.0 1.2 dynamic_slice.3
  9.3 0.6 compare_convert_fusion.1
  9.8 3.3 bitcast_convert_fusion
  13.1 6.2 %multiply_convert_fusion = bf16[4,1024,2048]{2,1,0:T(8,128)(2,1)} fusion(f32[1024,2048]{1,0:T(8,128)S(1)} %bitcast_convert_fusion, f32[4]{0:T(128)S(1)} %compare_convert_fusion.1), kind=kLoop, calls=%fused_computation | loop fusion | flops 16777216 | bytes 25165840 | tf_op jit(solution)/shard_map/convert_element_type | solution.py:54
  19.3 28.6 %copy.14 = bf16[4,1024,2048]{1,0,2:T(4,128)(2,1)} copy(bf16[4,1024,2048]{2,1,0:T(8,128)(2,1)} %multiply_convert_fusion) | data formatting | bytes 33554432
  47.9 17.0 %copy.16 = bf16[256,8,4,1024]{3,1,2,0:T(8,128)(2,1)} copy(bf16[256,8,4,1024]{3,2,1,0:T(4,128)(2,1)} %bitcast.38) | data formatting | bytes 33554432
  64.9 0.0 reduce-scatter.7.cloned.1.call-update
  64.9 0.0 copy-start.3
  64.9 0.0 all-gather.6.cloned.1.call-start
  65.0 0.5 all-gather.6.cloned.1.call-update
  65.5 0.0 all-gather.4.cloned.1.call-start
  65.6 0.0 copy-done.3
  65.6 180.7 %reduce-scatter.7.cloned.1.call-done = bf16[128,4096]{1,0:T(8,128)(2,1)} async-done(((bf16[2048,4096]{1,0:T(8,128)(2,1)}), bf16[128,4096]{1,0:T(8,128)(2,1)}) %reduce-scatter.7.cloned.1.call-update) | async-done | bytes 1048592
  246.3 1.8 reshape.41
  248.1 1.0 copy.15
  249.1 4.2 fusion.17
  253.3 1.7 fusion.18
  255.0 0.0 all-gather.4.cloned.1.call-update
  255.0 0.2 reduce-scatter.5.cloned.1.call-start
  255.2 0.6 fusion.16
  255.8 2.6 fusion.6
  258.4 0.0 all-gather.6.cloned.1.call-done
  258.5 0.0 copy-start.1
  258.5 12.5 %fusion.9 = bf16[768,2048]{1,0:T(8,128)(2,1)S(1)} fusion(bf16[1,2048,2048]{2,1,0:T(8,128)(2,1)} %all-gather.6.cloned.1.call-done, bf16[1,768,2048]{2,1,0:T(8,128)(2,1)} %param.10, f32[768]{0:T(1024)S(1)} %get-tuple-element.3, bf16[1,768,2048]{2,1,0:T(8,128)(2,1)} %param.9, f32[768]{0:T(1024)S(1)} %add_rsqrt_fusion), kind=kOutput, calls=%fused_computation.15 | convolution fusion | flops 6455033856 | bytes 17831936 | tf_op jit(solution)/shard_map/dot_general | solution.py:29
  271.0 9.4 %convolution_convert_fusion = bf16[2048,2048]{1,0:T(8,128)(2,1)} fusion(bf16[768,2048]{1,0:T(8,128)(2,1)S(1)} %fusion.9, bf16[1,768,2048]{2,1,0:T(8,128)(2,1)S(1)} %copy-done.1, f32[768]{0:T(1024)S(1)} %add_rsqrt_fusion), kind=kOutput, calls=%fused_computation.10 | convolution fusion | flops 6451363840 | bytes 14683136 | tf_op jit(solution)/shard_map/ti,tj->ij/dot_general | solution.py:39
  280.4 0.0 reduce-scatter.5.cloned.1.call-update
  280.4 5.7 %psum.7 = f32[]{:T(128)} all-reduce(f32[]{:T(128)} %get-tuple-element.4), channel_id=1, replica_groups=mesh['path'=16,'fsdp'=2] {'fsdp'}, use_global_device_ids=true, to_apply=%region_3.0 | all-reduce | flops 1 | bytes 8 | tf_op jit(solution)/shard_map/psum | solution.py:26
  286.8 97.3 %all-gather.4.cloned.1.call-done = bf16[4,1024,2048]{2,1,0:T(8,128)(2,1)} async-done(((bf16[4,1024,128]{2,1,0:T(8,128)(2,1)}), bf16[4,1024,2048]{2,1,0:T(8,128)(2,1)}) %all-gather.4.cloned.1.call-update) | async-done | bytes 16777232 | tf_op jit(solution)/shard_map/all_gather | solution.py:61
  384.1 43.3 %fusion = f32[1,1024,2048]{2,0,1:T(1,128)} fusion(bf16[4,1024,2048]{2,1,0:T(8,128)(2,1)} %all-gather.4.cloned.1.call-done, s32[]{:T(128)} %bitcast.5), kind=kOutput, calls=%fused_computation.1 | convolution fusion | flops 16777228 | bytes 25165828 | tf_op jit(solution)/shard_map/m,mrc->rc/dot_general | solution.py:62
  427.4 56.2 %reduce-scatter.5.cloned.1.call-done = bf16[1024,2048]{1,0:T(8,128)(2,1)} async-done(((bf16[2048,2048]{1,0:T(8,128)(2,1)}), bf16[1024,2048]{1,0:T(8,128)(2,1)}) %reduce-scatter.5.cloned.1.call-update) | async-done | bytes 4194320 | tf_op jit(solution)/shard_map/reduce_scatter | solution.py:38
  483.6 9.6 %fusion.10 = bf16[1,1024,2048]{2,1,0:T(8,128)(2,1)} fusion(f32[1,1024,2048]{2,0,1:T(1,128)} %fusion, f32[]{:T(128)S(6)} %sqrt.3, bf16[1024,2048]{1,0:T(8,128)(2,1)} %reduce-scatter.5.cloned.1.call-done, bf16[1,1024,2048]{2,1,0:T(8,128)(2,1)} %param.12), kind=kLoop, calls=%fused_computation.17 | loop fusion | flops 14680064 | bytes 20971524 | tf_op jit(solution)/shard_map/broadcast_in_dim | solution.py:65
  (7 shorter events, 0.0 us)
Async XLA Ops:
  8.0 238.3 %reduce-scatter.7.cloned.1.call-start = ((), (), s32[]{:S(2)}) async-start(), calls=%async_computation.5 | async-start | bytes 17825792
  64.9 0.7 copy-start.3
  64.9 193.5 %all-gather.6.cloned.1.call-start = ((), (), s32[]{:S(2)}) async-start(), calls=%async_computation.4 | async-start | bytes 12582912 | tf_op jit(solution)/shard_map/all_gather | solution.py:31
  65.5 318.6 %all-gather.4.cloned.1.call-start = ((), (), s32[]{:S(2)}) async-start(), calls=%async_computation.3 | async-start | bytes 17825792 | tf_op jit(solution)/shard_map/all_gather | solution.py:61
  253.3 5.1 %copy-start = (f32[4,1024,128]{2,1,0:T(8,128)}, f32[4,1024,128]{2,1,0:T(8,128)S(1)}, u32[]{:S(2)}) copy-start(f32[4,1024,128]{2,1,0:T(8,128)S(1)} %get-tuple-element.6) | copy-start | bytes 6291460
  253.3 1.9 copy-start.2
  255.0 228.6 %reduce-scatter.5.cloned.1.call-start = ((), (), s32[]{:S(2)}) async-start(), calls=%async_computation.2 | async-start | bytes 12582912 | tf_op jit(solution)/shard_map/reduce_scatter | solution.py:38
  258.5 12.5 %copy-start.1 = (bf16[1,768,2048]{2,1,0:T(8,128)(2,1)S(1)}, bf16[1,768,2048]{2,1,0:T(8,128)(2,1)}, u32[]{:S(2)}) copy-start(bf16[1,768,2048]{2,1,0:T(8,128)(2,1)} %param.9) | copy-start | bytes 9437188
Sparse Core Ops, SparseCore 0:
  65.0 181.2 reduce-scatter.6
Sparse Core Ops, SparseCore 1:
  66.9 106.5 all-gather.5
  255.1 129.0 all-gather.3
  386.3 97.3 reduce-scatter.4
where the time goes:
time: 502 us; the launch traced here: 501 us
  waiting for transfers between devices  335 us (67%)
  matrix products  65.2 us (13%)
  local copies, waits for them, and re-layouts  49.7 us (10%)
  other arithmetic  28.6 us (6%)
  between operations  16.4 us (3%)
  blocking collectives  5.69 us (1%)
    unnamed x5, waiting for transfers between devices  181 us
    all_gather x1, waiting for transfers between devices, per_device(): every_step = lax.all_gather(outer_step_b, 'path', axis=2, tiled=True)  97.3 us
    reduce_scatter x1, waiting for transfers between devices, per_device(): lax.psum_scatter(jnp.einsum('ti,tj->ij', columns, residual_rows, preferre...  56.2 us
    unnamed x12, local copies, waits for them, and re-layouts  48.5 us
    dot_general x1, matrix products, per_device(): jnp.einsum('m,mrc->rc', mine_hot.astype(jnp.bfloat16), every_step, prefer...  43.3 us
    dot_general x1, matrix products, per_device(): jnp.dot(columns, lax.all_gather(weights, 'fsdp', axis=0, tiled=True), pre...  12.5 us
  transfers between devices with their start and end apart: 4, of which 3 were waited for; matrix products, arithmetic and copies ran while one was open for 15% of the time, Pallas kernels for 0%

commit v1 on v0

v1 whole, which is shorter than its diff:
```python
import functools
import math

import jax
import jax.numpy as jnp
from jax import lax
from jax.sharding import PartitionSpec as P


def per_device(
    paths,
    shards,
    inputs,
    targets,
    token_ids,
    path_weights,
    stale_deltas,
    module_params,
    momentum,
    module_of_path,
    sharing_counts,
):
    modules, rows, width = module_params.shape
    weights = path_weights[0]
    width_in = inputs.shape[-1]
    pair = shards == 2
    swap = [(0, 1), (1, 0)]

    if pair:
        other_weights = lax.ppermute(weights, "fsdp", swap)
    else:
        all_weights = lax.all_gather(weights, "fsdp", axis=0, tiled=True)

    delta = stale_deltas[0]
    sent = jnp.stack([delta[:, p * width : (p + 1) * width] for p in range(paths)])
    arrived = lax.all_to_all(sent, "path", 0, 0, tiled=True)
    labels = jnp.arange(modules, dtype=jnp.int32)
    hot = (labels[:, None] == module_of_path[None, :]).astype(jnp.float32)
    total = jnp.sum(hot[:, :, None, None] * arrived.astype(jnp.float32)[None], axis=1)
    outer_grad = total / sharing_counts.astype(jnp.float32)[:, None, None]
    new_momentum = 0.9 * momentum + outer_grad
    outer_step = 0.7 * (outer_grad + 0.9 * new_momentum)
    new_params = module_params - outer_step
    outer_step_b = outer_step.astype(jnp.bfloat16)

    steps = jnp.sum(
        jnp.where(hot[:, :, None, None] != 0, outer_step_b.astype(jnp.float32)[:, None], 0.0),
        axis=0,
    ).astype(jnp.bfloat16)
    steps = lax.all_to_all(steps, "path", 0, 0, tiled=True)
    correction = jnp.concatenate([steps[p] for p in range(paths)], axis=1)

    values = inputs[0].astype(jnp.float32)
    scale = lax.rsqrt(jnp.mean(values * values, axis=-1, keepdims=True) + 1e-06)
    normed = (values * scale).astype(jnp.bfloat16)
    mask = (token_ids[0] != 0).astype(jnp.float32)
    count = lax.psum(jnp.sum(mask), "fsdp")

    def product(a, b):
        return jnp.dot(a, b, preferred_element_type=jnp.float32)

    if pair:
        me = lax.axis_index("fsdp")
        own = lax.dynamic_slice_in_dim(normed, me * rows, rows, 1)
        far = lax.dynamic_slice_in_dim(normed, (1 - me) * rows, rows, 1)
        projected = product(own, weights) + product(far, other_weights)
    else:
        projected = product(normed, all_weights)
    projected = projected / math.sqrt(width_in)
    residual_rows = ((projected - targets[0].astype(jnp.float32)) * mask[:, None]).astype(
        jnp.bfloat16
    )

    def gradient(columns):
        return jnp.einsum(
            "ti,tj->ij", columns, residual_rows, preferred_element_type=jnp.float32
        ).astype(jnp.bfloat16)

    if pair:
        far_grad = lax.ppermute(gradient(far), "fsdp", swap)
        grad = gradient(own).astype(jnp.float32) + far_grad.astype(jnp.float32)
    else:
        grad = lax.psum_scatter(
            gradient(normed), "fsdp", scatter_dimension=0, tiled=True
        ).astype(jnp.float32)
    inner = weights.astype(jnp.float32) - 0.25 * (grad / jnp.sqrt(count))
    next_weights = (inner - correction.astype(jnp.float32)).astype(jnp.bfloat16)[None]
    return (next_weights, new_params, new_momentum)


def solution(mesh):
    return jax.shard_map(
        functools.partial(per_device, mesh.shape["path"], mesh.shape["fsdp"]),
        mesh=mesh,
        in_specs=(
            P("path", "fsdp", None),
            P("path", "fsdp", None),
            P("path", "fsdp"),
            P("path", "fsdp", None),
            P("path", "fsdp", None),
            P(None, "fsdp", "path"),
            P(None, "fsdp", "path"),
            P(),
            P(),
        ),
        out_specs=(P("path", "fsdp", None), P(None, "fsdp", "path"), P(None, "fsdp", "path")),
        check_vma=False,
    )
```

time: 502 us -> 370 us (0.74)
  waiting for transfers between devices: 335 us -> 163 us
  blocking collectives: 5.69 us -> 91.4 us
  matrix products: 65.2 us -> 24.4 us
  starting transfers between devices: 0.35 us -> 30.6 us
  between operations: 16.4 us -> 1.56 us
  local copies, waits for them, and re-layouts: 49.7 us -> 38.9 us
  other arithmetic: 28.6 us -> 19.1 us
    unnamed x5 -> x0, waiting for transfers between devices: 181 us -> none
    all_gather x2 -> x0, waiting for transfers between devices: 97.3 us -> none  [the longest x1 97.3 us: per_device(): every_step = lax.all_gather(outer_step_b, 'path', axis=2, tiled=True)]
    psum x1, blocking collectives: 5.69 us -> 91.4 us  [per_device(): count = lax.psum(jnp.sum(mask), 'fsdp')]
    ppermute x0 -> x2, waiting for transfers between devices: none -> 85.3 us  [the longest x1 85.3 us: per_device(): other_weights = lax.ppermute(weights, 'fsdp', swap)]
    all_to_all x0 -> x2, waiting for transfers between devices: none -> 77.6 us  [the longest x1 77.6 us: per_device(): arrived = lax.all_to_all(sent, 'path', 0, 0, tiled=True)]
    reduce_scatter x1 -> x0, waiting for transfers between devices: 56.2 us -> none  [per_device(): lax.psum_scatter(jnp.einsum('ti,tj->ij', columns, residual_rows, preferre...]
    dot_general x3 -> x4, matrix products: 65.2 us -> 24.4 us  [the longest x2 14.6 us: gradient(): jnp.einsum('ti,tj->ij', columns, residual_rows, preferred_element_type=jn...]
    all_to_all x0 -> x2, starting transfers between devices: none -> 27.5 us  [the longest x1 20 us: per_device(): steps = lax.all_to_all(steps, 'path', 0, 0, tiled=True)]
  transfers between devices with their start and end apart: 4 -> 4, of which waited for: 3 -> 2; matrix products, arithmetic and copies ran while one was open for 15% -> 9% of each run, Pallas kernels for 0% -> 0%
where the time goes in v1:
time: 370 us; the launch traced here: 369 us
  waiting for transfers between devices  163 us (44%)
  blocking collectives  91.4 us (25%)
  local copies, waits for them, and re-layouts  38.9 us (11%)
  starting transfers between devices  30.6 us (8%)
  matrix products  24.4 us (7%)
  other arithmetic  19.1 us (5%)
    psum x1, blocking collectives, per_device(): count = lax.psum(jnp.sum(mask), 'fsdp')  91.4 us
    ppermute x1, waiting for transfers between devices, per_device(): other_weights = lax.ppermute(weights, 'fsdp', swap)  85.3 us
    all_to_all x1, waiting for transfers between devices, per_device(): arrived = lax.all_to_all(sent, 'path', 0, 0, tiled=True)  77.6 us
    unnamed x58, local copies, waits for them, and re-layouts  37.1 us
    all_to_all x1, starting transfers between devices, per_device(): steps = lax.all_to_all(steps, 'path', 0, 0, tiled=True)  20 us
    dot_general x2, matrix products, gradient(): jnp.einsum('ti,tj->ij', columns, residual_rows, preferred_element_type=jn...  14.6 us
    dot_general x2, matrix products, product(): return jnp.dot(a, b, preferred_element_type=jnp.float32)  9.88 us
    all_to_all x1, starting transfers between devices, per_device(): arrived = lax.all_to_all(sent, 'path', 0, 0, tiled=True)  7.57 us
  transfers between devices with their start and end apart: 4, of which 2 were waited for; matrix products, arithmetic and copies ran while one was open for 9% of the time, Pallas kernels for 0%

profile of v1, /device:TPU:0, one launch (start us, length us, event | category | flops | bytes accessed | tf_op | source)
XLA Modules:
  0.0 368.9 jit_solution(15779342759215341050)
XLA Ops:
  0.6 1.8 fusion.42
  2.5 1.7 fusion.41
  4.1 1.7 fusion.40
  5.8 1.7 fusion.39
  7.5 1.7 fusion.38
  9.1 1.7 fusion.37
  10.8 1.7 fusion.36
  12.5 1.7 fusion.35
  20.3 7.6 %all-to-all-start = ((bf16[16,1024,128]{2,1,0:T(8,128)(2,1)}), bf16[16,1024,128]{2,1,0:T(8,128)(2,1)}, u32[]{:S(2)}, u32[]{:S(2)}) async-start(bf16[16,1024,128]{2,1,0:T(8,128)(2,1)} %fusion.27), calls=%async_computation | async-start | bytes 8388608 | tf_op jit(solution)/shard_map/all_to_all | solution.py:36
  28.0 77.6 %all-to-all-done = bf16[16,1024,128]{2,1,0:T(8,128)(2,1)} async-done(((bf16[16,1024,128]{2,1,0:T(8,128)(2,1)}), bf16[16,1024,128]{2,1,0:T(8,128)(2,1)}, u32[]{:S(2)}, u32[]{:S(2)}) %all-to-all-start) | async-done | bytes 4194336 | tf_op jit(solution)/shard_map/all_to_all | solution.py:36
  105.6 3.0 convert_element_type.88
  108.7 5.3 %multiply_reduce_fusion = f32[4,1024,128]{2,1,0:T(8,128)S(1)} fusion(f32[16,1024,128]{2,1,0:T(8,128)S(1)} %convert_element_type.88, f32[4,16]{1,0:T(4,128)S(1)} %get-tuple-element.8), kind=kLoop, calls=%fused_computation.1 | loop fusion | flops 16252928 | bytes 10486016 | tf_op jit(solution)/shard_map/reduce_sum | solution.py:39
  114.0 1.9 fusion.10
  117.2 6.5 %select_reduce_fusion = bf16[16,1024,128]{2,1,0:T(8,128)(2,1)} fusion(f32[4,1024,128]{2,1,0:T(8,128)S(1)} %convert_convert_fusion, pred[4,16]{1,0:T(4,128)(4,1)S(1)} %get-tuple-element.7), kind=kLoop, calls=%fused_computation | loop fusion | flops 14680064 | bytes 6291520 | tf_op jit(solution)/shard_map/reduce_sum | solution.py:46
  123.8 20.0 %all-to-all-start.1 = ((bf16[16,1024,128]{2,1,0:T(8,128)(2,1)}), bf16[16,1024,128]{2,1,0:T(8,128)(2,1)}, u32[]{:S(2)}, u32[]{:S(2)}) async-start(bf16[16,1024,128]{2,1,0:T(8,128)(2,1)} %select_reduce_fusion), calls=%async_computation.1 | async-start | bytes 8388608 | tf_op jit(solution)/shard_map/all_to_all | solution.py:50
  143.7 1.6 collective-permute-start
  148.2 3.5 fusion.8
  151.6 85.3 %collective-permute-done = bf16[1024,2048]{1,0:T(8,128)(2,1)} collective-permute-done((bf16[1024,2048]{1,0:T(8,128)(2,1)}, bf16[1024,2048]{1,0:T(8,128)(2,1)}, u32[]{:S(2)}, u32[]{:S(2)}) %collective-permute-start) | collective-permute-done | bytes 4194336 | tf_op jit(solution)/shard_map/ppermute | solution.py:30
  236.9 6.4 %fusion.3 = bf16[768,2048]{1,0:T(8,128)(2,1)S(1)} fusion(f32[768,2048]{1,0:T(8,128)S(1)} %fusion.8, bf16[1024,2048]{1,0:T(8,128)(2,1)} %collective-permute-done, bf16[1,768,2048]{2,1,0:T(8,128)(2,1)S(1)} %copy-done.11, f32[768]{0:T(1024)S(1)} %get-tuple-element.3, bf16[768,2048]{1,0:T(8,128)(2,1)S(1)} %fusion.1, s32[]{:T(128)S(6)} %select_n.11), kind=kOutput, calls=%fused_computation.9 | convolution fusion | flops 3230662656 | bytes 18354180 | tf_op jit(solution)/shard_map/dot_general | solution.py:60
  243.4 5.1 %convolution_convert_fusion = bf16[1024,2048]{1,0:T(8,128)(2,1)} fusion(bf16[768,2048]{1,0:T(8,128)(2,1)S(1)} %fusion.3, bf16[768,2048]{1,0:T(8,128)(2,1)S(1)} %fusion.1, s32[]{:T(128)S(6)} %select_n.11), kind=kOutput, calls=%fused_computation.11 | convolution fusion | flops 3223322624 | bytes 8912900 | tf_op jit(solution)/shard_map/ti,tj->ij/dot_general | solution.py:75
  248.5 1.5 collective-permute-start.1
  250.0 91.4 %psum.7 = f32[]{:T(128)} all-reduce(f32[]{:T(128)} %get-tuple-element.4), channel_id=1, replica_groups=mesh['path'=16,'fsdp'=2] {'fsdp'}, use_global_device_ids=true, to_apply=%region_2.3 | all-reduce | flops 1 | bytes 8 | tf_op jit(solution)/shard_map/psum | solution.py:57
  342.0 1.2 fusion.26
  343.2 1.7 fusion.25
  344.8 1.0 fusion.24
  346.9 1.0 fusion.22
  348.0 1.0 fusion.21
  349.0 1.0 fusion.20
  351.1 1.0 fusion.18
  352.1 1.0 fusion.17
  355.3 1.0 fusion.14
  359.5 9.4 %fusion.4 = bf16[1,1024,2048]{2,1,0:T(8,128)(2,1)} fusion(bf16[1024,2048]{1,0:T(8,128)(2,1)S(1)} %fusion.11, f32[]{:T(128)S(6)} %sqrt.3, bf16[1024,2048]{1,0:T(8,128)(2,1)} %collective-permute-done.1, bf16[768,2048]{1,0:T(8,128)(2,1)} %copy-done.13, bf16[768,2048]{1,0:T(8,128)(2,1)S(1)} %copy-done.4, s32[]{:T(128)S(6)} %select_n.10, ...), kind=kOutput, calls=%fused_computation.10 | convolution fusion | flops 3244294144 | bytes 21495816 | tf_op jit(solution)/shard_map/ti,tj->ij/dot_general | solution.py:75
  (52 shorter events, 17.7 us)
Async XLA Ops:
  0.6 13.5 %copy-start.2 = (bf16[1,1024,2048]{2,1,0:T(8,128)(2,1)S(1)}, bf16[1,1024,2048]{2,1,0:T(8,128)(2,1)}, u32[]{:S(2)}) copy-start(bf16[1,1024,2048]{2,1,0:T(8,128)(2,1)} %param.13) | copy-start | bytes 12582916
  20.3 7.6 %copy-start.12 = (s32[4]{0:T(128)S(1)}, s32[4]{0:T(128)}, u32[]{:S(2)}) copy-start(s32[4]{0:T(128)} %param.17) | copy-start | bytes 52
  20.3 7.6 %copy-start.8 = (s32[16]{0:T(128)S(1)}, s32[16]{0:T(128)}, u32[]{:S(2)}) copy-start(s32[16]{0:T(128)} %param.16) | copy-start | bytes 196
  20.3 85.3 %all-to-all-start = ((bf16[16,1024,128]{2,1,0:T(8,128)(2,1)}), bf16[16,1024,128]{2,1,0:T(8,128)(2,1)}, u32[]{:S(2)}, u32[]{:S(2)}) async-start(bf16[16,1024,128]{2,1,0:T(8,128)(2,1)} %fusion.27), calls=%async_computation | async-start | bytes 8388608 | tf_op jit(solution)/shard_map/all_to_all | solution.py:36
  108.6 5.3 %copy-start.5 = (f32[4,1024,128]{2,1,0:T(8,128)S(1)}, f32[4,1024,128]{2,1,0:T(8,128)}, u32[]{:S(2)}) copy-start(f32[4,1024,128]{2,1,0:T(8,128)} %param.14) | copy-start | bytes 6291460
  108.6 5.3 %copy-start.6 = (f32[4,1024,128]{2,1,0:T(8,128)S(1)}, f32[4,1024,128]{2,1,0:T(8,128)}, u32[]{:S(2)}) copy-start(f32[4,1024,128]{2,1,0:T(8,128)} %param.15) | copy-start | bytes 6291460
  115.9 1.3 copy-start.1
  123.8 21.5 %copy-start.7 = (s32[1,768]{1,0:T(1,128)S(1)}, s32[1,768]{1,0:T(1,128)}, u32[]{:S(2)}) copy-start(s32[1,768]{1,0:T(1,128)} %param.11) | copy-start | bytes 9220
  123.8 22.2 %copy-start = (bf16[1,768,2048]{2,1,0:T(8,128)(2,1)S(1)}, bf16[1,768,2048]{2,1,0:T(8,128)(2,1)}, u32[]{:S(2)}) copy-start(bf16[1,768,2048]{2,1,0:T(8,128)(2,1)} %param.9) | copy-start | bytes 9437188
  123.8 218.2 %all-to-all-start.1 = ((bf16[16,1024,128]{2,1,0:T(8,128)(2,1)}), bf16[16,1024,128]{2,1,0:T(8,128)(2,1)}, u32[]{:S(2)}, u32[]{:S(2)}) async-start(bf16[16,1024,128]{2,1,0:T(8,128)(2,1)} %select_reduce_fusion), calls=%async_computation.1 | async-start | bytes 8388608 | tf_op jit(solution)/shard_map/all_to_all | solution.py:50
  143.7 93.2 %collective-permute-start = (bf16[1024,2048]{1,0:T(8,128)(2,1)}, bf16[1024,2048]{1,0:T(8,128)(2,1)}, u32[]{:S(2)}, u32[]{:S(2)}) collective-permute-start(bf16[1024,2048]{1,0:T(8,128)(2,1)} %bitcast.161), channel_id=1, source_target_pairs={{0,1},{1,0},{2,3},{3,2},{4,5},{5,4},{6,7},{7,6},{8,9},{9,8},{10,11... | collective-permute-start | bytes 12582920 | tf_op jit(solution)/shard_map/ppermute | solution.py:30
  146.0 2.2 copy-start.9
  148.2 95.2 %copy-start.3 = (bf16[768,2048]{1,0:T(8,128)(2,1)}, bf16[768,2048]{1,0:T(8,128)(2,1)S(1)}, u32[]{:S(2)}) copy-start(bf16[768,2048]{1,0:T(8,128)(2,1)S(1)} %fusion.1) | copy-start | bytes 9437188
  148.2 88.8 %copy-start.11 = (bf16[1,768,2048]{2,1,0:T(8,128)(2,1)S(1)}, bf16[1,768,2048]{2,1,0:T(8,128)(2,1)}, u32[]{:S(2)}) copy-start(bf16[1,768,2048]{2,1,0:T(8,128)(2,1)} %param.10) | copy-start | bytes 9437188
  243.4 5.1 %copy-start.13 = (bf16[768,2048]{1,0:T(8,128)(2,1)}, bf16[768,2048]{1,0:T(8,128)(2,1)S(1)}, u32[]{:S(2)}) copy-start(bf16[768,2048]{1,0:T(8,128)(2,1)S(1)} %fusion.3) | copy-start | bytes 9437188
  248.5 110.9 %collective-permute-start.1 = (bf16[1024,2048]{1,0:T(8,128)(2,1)}, bf16[1024,2048]{1,0:T(8,128)(2,1)}, u32[]{:S(2)}, u32[]{:S(2)}) collective-permute-start(bf16[1024,2048]{1,0:T(8,128)(2,1)} %convolution_convert_fusion), channel_id=1, source_target_pairs={{0,1},{1,0},{2,3},{3,2},{4,5},{5,4},{6,7},{7,6},{8,9},{9,8},{10,11... | collective-permute-start | bytes 12582920 | tf_op jit(solution)/shard_map/ppermute | solution.py:80
  342.0 17.5 %copy-start.4 = (bf16[768,2048]{1,0:T(8,128)(2,1)S(1)}, bf16[768,2048]{1,0:T(8,128)(2,1)}, u32[]{:S(2)}) copy-start(bf16[768,2048]{1,0:T(8,128)(2,1)} %copy-done.3) | copy-start | bytes 9437188
  342.0 17.5 %copy-start.10 = (bf16[1,1024,2048]{2,1,0:T(8,128)(2,1)S(1)}, bf16[1,1024,2048]{2,1,0:T(8,128)(2,1)}, u32[]{:S(2)}) copy-start(bf16[1,1024,2048]{2,1,0:T(8,128)(2,1)} %param.12) | copy-start | bytes 12582916

commit v2 on v1

v2 whole, which is shorter than its diff:
```python
import functools
import math

import jax
import jax.numpy as jnp
from jax import lax
from jax.experimental import pallas as pl
from jax.experimental.pallas import tpu as pltpu
from jax.sharding import PartitionSpec as P


def cost(flops, traffic):
    return pl.CostEstimate(flops=flops, bytes_accessed=traffic, transcendentals=0)


def split_columns(delta, paths):
    rows, columns = delta.shape
    width = columns // paths
    if width % 128:
        return jnp.stack([delta[:, p * width : (p + 1) * width] for p in range(paths)])

    def kernel(delta_ref, out_ref):
        out_ref[0] = delta_ref[...]

    return pl.pallas_call(
        kernel,
        grid=(paths,),
        in_specs=[pl.BlockSpec((rows, width), lambda p: (0, p))],
        out_specs=pl.BlockSpec((1, rows, width), lambda p: (p, 0, 0)),
        out_shape=jax.ShapeDtypeStruct((paths, rows, width), delta.dtype),
        cost_estimate=cost(0, 4 * delta.size),
    )(delta)


def outer_update(arrived, module_params, momentum, module_of_path, sharing_counts):
    paths, rows, width = arrived.shape
    modules = module_params.shape[0]
    tile = 128 if rows % 128 == 0 else rows

    def kernel(
        module_ref, count_ref, arrived_ref, params_ref, momentum_ref,
        params_out, momentum_out, steps_out, total,
    ):
        total[...] = jnp.zeros_like(total)
        for p in range(paths):
            m = module_ref[p]
            total[m] = total[m] + arrived_ref[p].astype(jnp.float32)
        for m in range(modules):
            shared = jnp.full((tile, width), count_ref[m], jnp.int32).astype(jnp.float32)
            outer_grad = total[m] / shared
            new_momentum = 0.9 * momentum_ref[m] + outer_grad
            outer_step = 0.7 * (outer_grad + 0.9 * new_momentum)
            params_out[m] = params_ref[m] - outer_step
            momentum_out[m] = new_momentum
            total[m] = outer_step
        for p in range(paths):
            steps_out[p] = total[module_ref[p]].astype(jnp.bfloat16)

    def block(n):
        return pl.BlockSpec((n, tile, width), lambda r: (0, r, 0))

    table = pl.BlockSpec(memory_space=pltpu.SMEM)
    state = jax.ShapeDtypeStruct(module_params.shape, jnp.float32)
    return pl.pallas_call(
        kernel,
        grid=(rows // tile,),
        in_specs=[table, table, block(paths), block(modules), block(modules)],
        out_specs=[block(modules), block(modules), block(paths)],
        out_shape=[state, state, jax.ShapeDtypeStruct(arrived.shape, jnp.bfloat16)],
        scratch_shapes=[pltpu.VMEM((modules, tile, width), jnp.float32)],
        compiler_params=pltpu.CompilerParams(vmem_limit_bytes=24 * 2**20),
        cost_estimate=cost(4 * arrived.size, 4 * arrived.size + 16 * module_params.size),
    )(module_of_path, sharing_counts, arrived, module_params, momentum)


def finish(weights, own_grad, far_grad, steps, count):
    paths, rows, width = steps.shape
    if width % 128:
        correction = jnp.concatenate([steps[p] for p in range(paths)], axis=1)
        grad = own_grad.astype(jnp.float32) + far_grad.astype(jnp.float32)
        inner = weights.astype(jnp.float32) - 0.25 * (grad / jnp.sqrt(count))
        return (inner - correction.astype(jnp.float32)).astype(jnp.bfloat16)

    def kernel(root_ref, weights_ref, own_ref, far_ref, steps_ref, out_ref):
        grad = own_ref[...].astype(jnp.float32) + far_ref[...].astype(jnp.float32)
        grad = grad / jnp.broadcast_to(root_ref[...], grad.shape)
        inner = weights_ref[...].astype(jnp.float32) - 0.25 * grad
        out_ref[...] = (inner - steps_ref[0].astype(jnp.float32)).astype(jnp.bfloat16)

    column = pl.BlockSpec((rows, width), lambda p: (0, p))
    return pl.pallas_call(
        kernel,
        grid=(paths,),
        in_specs=[
            pl.BlockSpec((1, width), lambda p: (0, 0)),
            column,
            column,
            column,
            pl.BlockSpec((1, rows, width), lambda p: (p, 0, 0)),
        ],
        out_specs=column,
        out_shape=jax.ShapeDtypeStruct(weights.shape, jnp.bfloat16),
        compiler_params=pltpu.CompilerParams(vmem_limit_bytes=24 * 2**20),
        cost_estimate=cost(6 * weights.size, 10 * weights.size),
    )(jnp.full((1, width), jnp.sqrt(count), jnp.float32), weights, own_grad, far_grad, steps)


def per_device(
    paths,
    shards,
    inputs,
    targets,
    token_ids,
    path_weights,
    stale_deltas,
    module_params,
    momentum,
    module_of_path,
    sharing_counts,
):
    rows = path_weights.shape[1]
    weights = path_weights[0]
    width_in = inputs.shape[-1]
    pair = shards == 2
    swap = [(0, 1), (1, 0)]

    mask = (token_ids[0] != 0).astype(jnp.float32)
    if pair:
        counted = jnp.full((8, 128), jnp.sum(mask), jnp.float32)
        count = (counted + lax.ppermute(counted, "fsdp", swap))[0, 0]
        other_weights = lax.ppermute(weights, "fsdp", swap)
    else:
        count = lax.psum(jnp.sum(mask), "fsdp")
        all_weights = lax.all_gather(weights, "fsdp", axis=0, tiled=True)

    arrived = lax.all_to_all(split_columns(stale_deltas[0], paths), "path", 0, 0, tiled=True)

    values = inputs[0].astype(jnp.float32)
    scale = lax.rsqrt(jnp.mean(values * values, axis=-1, keepdims=True) + 1e-06)
    normed = (values * scale).astype(jnp.bfloat16)

    def product(a, b):
        return jnp.dot(a, b, preferred_element_type=jnp.float32)

    if pair:
        me = lax.axis_index("fsdp")
        own = lax.dynamic_slice_in_dim(normed, me * rows, rows, 1)
        far = lax.dynamic_slice_in_dim(normed, (1 - me) * rows, rows, 1)
        projected = product(own, weights) + product(far, other_weights)
    else:
        projected = product(normed, all_weights)
    projected = projected / math.sqrt(width_in)
    residual_rows = ((projected - targets[0].astype(jnp.float32)) * mask[:, None]).astype(
        jnp.bfloat16
    )

    def gradient(columns):
        return jnp.einsum(
            "ti,tj->ij", columns, residual_rows, preferred_element_type=jnp.float32
        ).astype(jnp.bfloat16)

    if pair:
        sent_grad, arrived = lax.optimization_barrier((gradient(far), arrived))
        far_grad = lax.ppermute(sent_grad, "fsdp", swap)
        own_grad = gradient(own)
    else:
        own_grad = lax.psum_scatter(
            gradient(normed), "fsdp", scatter_dimension=0, tiled=True
        )
        far_grad = jnp.zeros_like(own_grad)

    new_params, new_momentum, steps = outer_update(
        arrived, module_params, momentum, module_of_path, sharing_counts
    )
    steps = lax.all_to_all(steps, "path", 0, 0, tiled=True)
    next_weights = finish(weights, own_grad, far_grad, steps, count)[None]
    return (next_weights, new_params, new_momentum)


def solution(mesh):
    return jax.shard_map(
        functools.partial(per_device, mesh.shape["path"], mesh.shape["fsdp"]),
        mesh=mesh,
        in_specs=(
            P("path", "fsdp", None),
            P("path", "fsdp", None),
            P("path", "fsdp"),
            P("path", "fsdp", None),
            P("path", "fsdp", None),
            P(None, "fsdp", "path"),
            P(None, "fsdp", "path"),
            P(),
            P(),
        ),
        out_specs=(P("path", "fsdp", None), P(None, "fsdp", "path"), P(None, "fsdp", "path")),
        check_vma=False,
    )
```

time: 370 us -> 266 us (0.72)
  blocking collectives: 91.4 us -> 0 us
  Pallas kernels: 0 us -> 29.7 us
  local copies, waits for them, and re-layouts: 38.9 us -> 15.8 us
  other arithmetic: 19.1 us -> 2.41 us
  starting transfers between devices: 30.6 us -> 17.5 us
  waiting for transfers between devices: 163 us -> 176 us
    psum x1 -> x0, blocking collectives: 91.4 us -> none  [per_device(): count = lax.psum(jnp.sum(mask), 'fsdp')]
    ppermute x1 -> x2, waiting for transfers between devices: 0.01 us -> 90.4 us  [the longest x1 90.4 us: per_device(): count = (counted + lax.ppermute(counted, 'fsdp', swap))[0, 0]]
    all_to_all x1, waiting for transfers between devices: 77.6 us -> 0.01 us  [per_device(): lax.all_to_all(split_columns(stale_deltas[0], paths), 'path', 0, 0, tiled...]
    pallas_call x0 -> x3, Pallas kernels: none -> 29.7 us  [the longest x1 12.3 us: finish(): pl.pallas_call(kernel, grid=(paths,), in_specs=[pl.BlockSpec((1, width),...]
    unnamed x58 -> x32, local copies, waits for them, and re-layouts: 37.1 us -> 14.7 us
    all_to_all x1, starting transfers between devices: 20 us -> 6.06 us  [per_device(): steps = lax.all_to_all(steps, 'path', 0, 0, tiled=True)]
    reduce_sum x2 -> x0, other arithmetic: 11.9 us -> none  [the longest x1 6.54 us: per_device(): jnp.sum(jnp.where(hot[:, :, None, None] != 0, outer_step_b.astype(jnp.flo...]
  transfers between devices with their start and end apart: 4 -> 5, of which waited for: 2 -> 2; matrix products, arithmetic and copies ran while one was open for 9% -> 10% of each run, Pallas kernels for 0% -> 0%
where the time goes in v2:
time: 266 us; the launch traced here: 265 us
  waiting for transfers between devices  176 us (66%)
  Pallas kernels  29.7 us (11%)
  matrix products  22 us (8%)
  starting transfers between devices  17.5 us (7%)
  local copies, waits for them, and re-layouts  15.8 us (6%)
    ppermute x1, waiting for transfers between devices, per_device(): count = (counted + lax.ppermute(counted, 'fsdp', swap))[0, 0]  90.4 us
    ppermute x1, waiting for transfers between devices, per_device(): other_weights = lax.ppermute(weights, 'fsdp', swap)  85.4 us
    unnamed x32, local copies, waits for them, and re-layouts  14.7 us
    pallas_call x1, Pallas kernels, finish(): pl.pallas_call(kernel, grid=(paths,), in_specs=[pl.BlockSpec((1, width),...  12.3 us
    dot_general x2, matrix products, gradient(): jnp.einsum('ti,tj->ij', columns, residual_rows, preferred_element_type=jn...  12.1 us
    pallas_call x1, Pallas kernels, split_columns(): pl.pallas_call(kernel, grid=(paths,), in_specs=[pl.BlockSpec((rows, width...  10.1 us
    dot_general x2, matrix products, product(): return jnp.dot(a, b, preferred_element_type=jnp.float32)  9.87 us
    all_to_all x1, starting transfers between devices, per_device(): lax.all_to_all(split_columns(stale_deltas[0], paths), 'path', 0, 0, tiled...  7.7 us
  transfers between devices with their start and end apart: 5, of which 2 were waited for; matrix products, arithmetic and copies ran while one was open for 10% of the time, Pallas kernels for 0%

profile of v2, /device:TPU:0, one launch (start us, length us, event | category | flops | bytes accessed | tf_op | source)
XLA Modules:
  0.0 264.5 jit_solution(14631289856694808895)
XLA Ops:
  0.6 10.1 %shard_map.112 = bf16[16,1024,128]{2,1,0:T(8,128)(2,1)} custom-call(bf16[1024,2048]{1,0:T(8,128)(2,1)} %bitcast.18), custom_call_target="tpu_custom_call" | custom-call | bytes 8388608 | tf_op jit(solution)/shard_map/pallas_call | solution.py:25
  10.7 7.7 %all-to-all-start = ((bf16[16,1024,128]{2,1,0:T(8,128)(2,1)}), bf16[16,1024,128]{2,1,0:T(8,128)(2,1)}, u32[]{:S(2)}, u32[]{:S(2)}) async-start(bf16[16,1024,128]{2,1,0:T(8,128)(2,1)} %shard_map.112), calls=%async_computation | async-start | bytes 8388608 | tf_op jit(solution)/shard_map/all_to_all | solution.py:136
  18.4 1.6 collective-permute-start.1
  20.0 0.6 fusion.9
  20.6 0.7 fusion
  21.3 0.6 fusion.1
  21.9 0.9 copy-done.1
  22.8 3.5 %fusion.7 = f32[768,2048]{1,0:T(8,128)S(1)} fusion(bf16[768,2048]{1,0:T(8,128)(2,1)S(1)} %fusion.1, s32[]{:T(128)S(6)} %select_n.6, bf16[1,1024,2048]{2,1,0:T(8,128)(2,1)S(1)} %copy-done.1), kind=kOutput, calls=%fused_computation.12 | convolution fusion | flops 3221225472 | bytes 12058628 | tf_op jit(solution)/shard_map/dot_general | solution.py:143
  26.2 85.4 %collective-permute-done.1 = bf16[1024,2048]{1,0:T(8,128)(2,1)} collective-permute-done((bf16[1024,2048]{1,0:T(8,128)(2,1)}, bf16[1024,2048]{1,0:T(8,128)(2,1)}, u32[]{:S(2)}, u32[]{:S(2)}) %collective-permute-start.1) | collective-permute-done | bytes 4194336 | tf_op jit(solution)/shard_map/ppermute | solution.py:131
  111.6 6.4 %fusion.3 = bf16[768,2048]{1,0:T(8,128)(2,1)S(1)} fusion(f32[768,2048]{1,0:T(8,128)S(1)} %fusion.7, bf16[1024,2048]{1,0:T(8,128)(2,1)} %collective-permute-done.1, bf16[1,768,2048]{2,1,0:T(8,128)(2,1)S(1)} %copy-done.14, f32[768]{0:T(1024)S(1)} %get-tuple-element.13, bf16[768,2048]{1,0:T(8,128)(2,1)S(1)} %fusion.1, s32[]{:T(128)S(6)} %select_n.7), kind=kOutput, calls=%fused_computation.6 | convolution fusion | flops 3230662656 | bytes 18354180 | tf_op jit(solution)/shard_map/dot_general | solution.py:143
  118.0 1.6 copy-done.15
  119.7 5.1 %convolution_convert_fusion = bf16[1024,2048]{1,0:T(8,128)(2,1)} fusion(bf16[768,2048]{1,0:T(8,128)(2,1)S(1)} %fusion.3, bf16[768,2048]{1,0:T(8,128)(2,1)S(1)} %fusion.1, s32[]{:T(128)S(6)} %select_n.7), kind=kOutput, calls=%fused_computation.7 | convolution fusion | flops 3223322624 | bytes 8912900 | tf_op jit(solution)/shard_map/ti,tj->ij/dot_general | solution.py:158
  124.8 0.0 all-to-all-done.arrived_ref
  124.8 0.0 copy-start.7
  124.9 1.6 copy-done.7
  126.4 7.4 %shard_map.113 = (f32[4,1024,128]{2,1,0:T(8,128)}, f32[4,1024,128]{2,1,0:T(8,128)}, bf16[16,1024,128]{2,1,0:T(8,128)(2,1)S(1)}) custom-call(s32[16]{0:T(128)S(1)} %copy-done.8, s32[4]{0:T(128)S(1)} %copy-done.9, bf16[16,1024,128]{2,1,0:T(8,128)(2,1)} %all-to-all-done.arrived_ref, f32[4,1024,128]{2,1,0:T(8,128)S(1)} %copy-done.6, f32[4,1024,128]{2,1,0:T(8,128)S(1)} %copy-done.7), custom_call_target="tpu_custom_call" | custom-call | flops 8388608 | bytes 16777216 | tf_op jit(solution)/shard_map/pallas_call | solution.py:64
  133.8 2.0 copy-done
  135.8 6.1 %all-to-all-start.1 = ((bf16[16,1024,128]{2,1,0:T(8,128)(2,1)}), bf16[16,1024,128]{2,1,0:T(8,128)(2,1)}, u32[]{:S(2)}, u32[]{:S(2)}) async-start(bf16[16,1024,128]{2,1,0:T(8,128)(2,1)} %copy-done), calls=%async_computation.1 | async-start | bytes 8388608 | tf_op jit(solution)/shard_map/all_to_all | solution.py:175
  141.8 1.6 collective-permute-start.2
  143.4 0.6 broadcast_in_dim.11
  144.0 0.6 collective-permute-start
  144.6 90.4 %collective-permute-done = f32[8,128]{1,0:T(8,128)S(1)} collective-permute-done((f32[8,128]{1,0:T(8,128)S(1)}, f32[8,128]{1,0:T(8,128)S(1)}, u32[]{:S(2)}, u32[]{:S(2)}) %collective-permute-start) | collective-permute-done | bytes 4128 | tf_op jit(solution)/shard_map/ppermute | solution.py:130
  235.0 0.6 broadcast_add_fusion
  235.6 0.5 slice.3
  236.8 6.9 %convolution_convert_fusion.1.own_ref = bf16[1024,2048]{1,0:T(8,128)(2,1)} fusion(bf16[768,2048]{1,0:T(8,128)(2,1)} %copy-done.15, bf16[768,2048]{1,0:T(8,128)(2,1)S(1)} %copy-done.12, s32[]{:T(128)S(6)} %select_n.6), kind=kOutput, calls=%fused_computation.8 | convolution fusion | flops 3223322624 | bytes 8912900 | tf_op jit(solution)/shard_map/ti,tj->ij/dot_general | solution.py:158
  243.7 0.0 collective-permute-done.2.far_ref
  243.7 2.0 copy-done.3
  245.7 0.0 all-to-all-done.1.steps_ref
  245.7 2.2 copy-done.2
  247.9 2.2 copy-done.4
  250.1 2.2 copy-done.5
  252.3 12.3 %shard_map.114 = bf16[1024,2048]{1,0:T(8,128)(2,1)} custom-call(f32[1,128]{1,0:T(1,128)S(1)} %broadcast_in_dim.12.root_ref, bf16[1024,2048]{1,0:T(8,128)(2,1)S(1)} %bitcast.17, bf16[1024,2048]{1,0:T(8,128)(2,1)S(1)} %copy-done.5, bf16[1024,2048]{1,0:T(8,128)(2,1)S(1)} %copy-done.4, bf16[16,1024,128]{2,1,0:T(8,128)(2,1)} %all-to-all-done.1.steps_ref), custom_call_target="tpu_custom_call" | custom-call | flops 12582912 | bytes 20971520 | tf_op jit(solution)/shard_map/pallas_call | solution.py:91
  (25 shorter events, 0.1 us)
Async XLA Ops:
  10.7 9.3 %copy-start.13 = (s32[1,768]{1,0:T(1,128)S(1)}, s32[1,768]{1,0:T(1,128)}, u32[]{:S(2)}) copy-start(s32[1,768]{1,0:T(1,128)} %param.11) | copy-start | bytes 9220
  10.7 9.9 %copy-start.10 = (bf16[1,768,2048]{2,1,0:T(8,128)(2,1)S(1)}, bf16[1,768,2048]{2,1,0:T(8,128)(2,1)}, u32[]{:S(2)}) copy-start(bf16[1,768,2048]{2,1,0:T(8,128)(2,1)} %param.9) | copy-start | bytes 9437188
  10.7 114.1 %all-to-all-start = ((bf16[16,1024,128]{2,1,0:T(8,128)(2,1)}), bf16[16,1024,128]{2,1,0:T(8,128)(2,1)}, u32[]{:S(2)}, u32[]{:S(2)}) async-start(bf16[16,1024,128]{2,1,0:T(8,128)(2,1)} %shard_map.112), calls=%async_computation | async-start | bytes 8388608 | tf_op jit(solution)/shard_map/all_to_all | solution.py:136
  18.4 93.2 %collective-permute-start.1 = (bf16[1024,2048]{1,0:T(8,128)(2,1)}, bf16[1024,2048]{1,0:T(8,128)(2,1)}, u32[]{:S(2)}, u32[]{:S(2)}) collective-permute-start(bf16[1024,2048]{1,0:T(8,128)(2,1)} %bitcast.16), channel_id=1, source_target_pairs={{0,1},{1,0},{2,3},{3,2},{4,5},{5,4},{6,7},{7,6},{8,9},{9,8},{10,11... | collective-permute-start | bytes 12582920 | tf_op jit(solution)/shard_map/ppermute | solution.py:131
  20.6 2.2 copy-start.1
  22.8 95.3 %copy-start.11 = (bf16[768,2048]{1,0:T(8,128)(2,1)}, bf16[768,2048]{1,0:T(8,128)(2,1)S(1)}, u32[]{:S(2)}) copy-start(bf16[768,2048]{1,0:T(8,128)(2,1)S(1)} %fusion.1) | copy-start | bytes 9437188
  22.8 88.8 %copy-start.14 = (bf16[1,768,2048]{2,1,0:T(8,128)(2,1)S(1)}, bf16[1,768,2048]{2,1,0:T(8,128)(2,1)}, u32[]{:S(2)}) copy-start(bf16[1,768,2048]{2,1,0:T(8,128)(2,1)} %param.10) | copy-start | bytes 9437188
  118.0 1.6 copy-start.15
  119.7 5.1 %copy-start.6 = (f32[4,1024,128]{2,1,0:T(8,128)S(1)}, f32[4,1024,128]{2,1,0:T(8,128)}, u32[]{:S(2)}) copy-start(f32[4,1024,128]{2,1,0:T(8,128)} %params_ref.1) | copy-start | bytes 6291460
  119.7 5.1 %copy-start.8 = (s32[16]{0:T(128)S(1)}, s32[16]{0:T(128)}, u32[]{:S(2)}) copy-start(s32[16]{0:T(128)} %module_ref.1) | copy-start | bytes 196
  119.7 5.2 %copy-start.9 = (s32[4]{0:T(128)S(1)}, s32[4]{0:T(128)}, u32[]{:S(2)}) copy-start(s32[4]{0:T(128)} %count_ref.1) | copy-start | bytes 52
  124.8 1.6 copy-start.7
  133.8 2.0 copy-start
  135.8 101.0 %copy-start.12 = (bf16[768,2048]{1,0:T(8,128)(2,1)S(1)}, bf16[768,2048]{1,0:T(8,128)(2,1)}, u32[]{:S(2)}) copy-start(bf16[768,2048]{1,0:T(8,128)(2,1)} %copy-done.11) | copy-start | bytes 9437188
  135.8 109.9 %all-to-all-start.1 = ((bf16[16,1024,128]{2,1,0:T(8,128)(2,1)}), bf16[16,1024,128]{2,1,0:T(8,128)(2,1)}, u32[]{:S(2)}, u32[]{:S(2)}) async-start(bf16[16,1024,128]{2,1,0:T(8,128)(2,1)} %copy-done), calls=%async_computation.1 | async-start | bytes 8388608 | tf_op jit(solution)/shard_map/all_to_all | solution.py:175
  141.8 101.9 %collective-permute-start.2 = (bf16[1024,2048]{1,0:T(8,128)(2,1)}, bf16[1024,2048]{1,0:T(8,128)(2,1)S(1)}, u32[]{:S(2)}, u32[]{:S(2)}) collective-permute-start(bf16[1024,2048]{1,0:T(8,128)(2,1)} %convolution_convert_fusion), channel_id=1, source_target_pairs={{0,1},{1,0},{2,3},{3,2},{4,5},{5,4},{6,7},{7,6},{8,9},{9,8},{10,11... | collective-permute-start | bytes 12582920 | tf_op jit(solution)/shard_map/ppermute | solution.py:164
  144.0 91.0 %collective-permute-start = (f32[8,128]{1,0:T(8,128)S(1)}, f32[8,128]{1,0:T(8,128)S(1)}, u32[]{:S(2)}, u32[]{:S(2)}) collective-permute-start(f32[8,128]{1,0:T(8,128)S(1)} %broadcast_in_dim.11), channel_id=1, source_target_pairs={{0,1},{1,0},{2,3},{3,2},{4,5},{5,4},{6,7},{7,6},{8,9},{9,8},{10,11... | collective-permute-start | bytes 12296 | tf_op jit(solution)/shard_map/ppermute | solution.py:130
  243.7 2.0 copy-start.3
  245.7 2.2 copy-start.2
  247.9 2.2 copy-start.4
  250.1 2.2 copy-start.5

commit v3 on v2

--- a/solution.py
+++ b/solution.py
@@ -19,15 +19,19 @@
     if width % 128:
         return jnp.stack([delta[:, p * width : (p + 1) * width] for p in range(paths)])
 
+    group = math.gcd(paths, 4)
+
     def kernel(delta_ref, out_ref):
-        out_ref[0] = delta_ref[...]
+        for g in range(group):
+            out_ref[g] = delta_ref[:, g * width : (g + 1) * width]
 
     return pl.pallas_call(
         kernel,
-        grid=(paths,),
-        in_specs=[pl.BlockSpec((rows, width), lambda p: (0, p))],
-        out_specs=pl.BlockSpec((1, rows, width), lambda p: (p, 0, 0)),
+        grid=(paths // group,),
+        in_specs=[pl.BlockSpec((rows, group * width), lambda p: (0, p))],
+        out_specs=pl.BlockSpec((group, rows, width), lambda p: (p, 0, 0)),
         out_shape=jax.ShapeDtypeStruct((paths, rows, width), delta.dtype),
+        compiler_params=pltpu.CompilerParams(vmem_limit_bytes=48 * 2**20),
         cost_estimate=cost(0, 4 * delta.size),
     )(delta)
 
@@ -68,41 +72,63 @@
         out_specs=[block(modules), block(modules), block(paths)],
         out_shape=[state, state, jax.ShapeDtypeStruct(arrived.shape, jnp.bfloat16)],
         scratch_shapes=[pltpu.VMEM((modules, tile, width), jnp.float32)],
-        compiler_params=pltpu.CompilerParams(vmem_limit_bytes=24 * 2**20),
+        compiler_params=pltpu.CompilerParams(vmem_limit_bytes=48 * 2**20),
         cost_estimate=cost(4 * arrived.size, 4 * arrived.size + 16 * module_params.size),
     )(module_of_path, sharing_counts, arrived, module_params, momentum)
 
 
-def finish(weights, own_grad, far_grad, steps, count):
+def finish(weights, own_grads, far_grads, steps, count):
     paths, rows, width = steps.shape
-    if width % 128:
+    parts = len(own_grads)
+    if width % 128 or paths % parts:
+        own_grad = jnp.concatenate(own_grads, axis=1)
+        far_grad = jnp.concatenate(far_grads, axis=1)
         correction = jnp.concatenate([steps[p] for p in range(paths)], axis=1)
         grad = own_grad.astype(jnp.float32) + far_grad.astype(jnp.float32)
         inner = weights.astype(jnp.float32) - 0.25 * (grad / jnp.sqrt(count))
         return (inner - correction.astype(jnp.float32)).astype(jnp.bfloat16)
 
-    def kernel(root_ref, weights_ref, own_ref, far_ref, steps_ref, out_ref):
-        grad = own_ref[...].astype(jnp.float32) + far_ref[...].astype(jnp.float32)
-        grad = grad / jnp.broadcast_to(root_ref[...], grad.shape)
-        inner = weights_ref[...].astype(jnp.float32) - 0.25 * grad
-        out_ref[...] = (inner - steps_ref[0].astype(jnp.float32)).astype(jnp.bfloat16)
-
-    column = pl.BlockSpec((rows, width), lambda p: (0, p))
+    group = math.gcd(paths // parts, 4)
+    turns = paths // parts // group
+    wide = group * width
+
+    def kernel(root_ref, weights_ref, steps_ref, *refs):
+        out_ref = refs[-1]
+        root = jnp.broadcast_to(root_ref[...], (rows, width))
+        for part in range(parts):
+            own_ref, far_ref = refs[2 * part : 2 * part + 2]
+
+            @pl.when(pl.program_id(0) // turns == part)
+            def _():
+                for g in range(group):
+                    at = slice(g * width, (g + 1) * width)
+                    grad = own_ref[:, at].astype(jnp.float32) + far_ref[:, at].astype(jnp.float32)
+                    inner = weights_ref[:, at].astype(jnp.float32) - 0.25 * (grad / root)
+                    new = inner - steps_ref[g].astype(jnp.float32)
+                    out_ref[:, at] = new.astype(jnp.bfloat16)
+
+    def within(part):
+        return lambda p: (0, jnp.clip(p - part * turns, 0, turns - 1))
+
+    column = pl.BlockSpec((rows, wide), lambda p: (0, p))
+    pieces, grads = [], []
+    for part in range(parts):
+        pieces += [pl.BlockSpec((rows, wide), within(part))] * 2
+        grads += [own_grads[part], far_grads[part]]
     return pl.pallas_call(
         kernel,
-        grid=(paths,),
+        grid=(parts * turns,),
         in_specs=[
             pl.BlockSpec((1, width), lambda p: (0, 0)),
             column,
-            column,
-            column,
-            pl.BlockSpec((1, rows, width), lambda p: (p, 0, 0)),
+            pl.BlockSpec((group, rows, width), lambda p: (p, 0, 0)),
+            *pieces,
         ],
         out_specs=column,
         out_shape=jax.ShapeDtypeStruct(weights.shape, jnp.bfloat16),
-        compiler_params=pltpu.CompilerParams(vmem_limit_bytes=24 * 2**20),
+        compiler_params=pltpu.CompilerParams(vmem_limit_bytes=48 * 2**20),
         cost_estimate=cost(6 * weights.size, 10 * weights.size),
-    )(jnp.full((1, width), jnp.sqrt(count), jnp.float32), weights, own_grad, far_grad, steps)
+    )(jnp.full((1, width), jnp.sqrt(count), jnp.float32), weights, steps, *grads)
 
 
 def per_device(
@@ -128,7 +154,9 @@
     if pair:
         counted = jnp.full((8, 128), jnp.sum(mask), jnp.float32)
         count = (counted + lax.ppermute(counted, "fsdp", swap))[0, 0]
-        other_weights = lax.ppermute(weights, "fsdp", swap)
+        half = weights.shape[1] // 2
+        left, right = weights[:, :half], weights[:, half:]
+        far_left = lax.ppermute(left, "fsdp", swap)
     else:
         count = lax.psum(jnp.sum(mask), "fsdp")
         all_weights = lax.all_gather(weights, "fsdp", axis=0, tiled=True)
@@ -141,39 +169,43 @@
 
     def product(a, b):
         return jnp.dot(a, b, preferred_element_type=jnp.float32)
+
+    def residual(projected, wanted):
+        projected = projected / math.sqrt(width_in)
+        return ((projected - wanted.astype(jnp.float32)) * mask[:, None]).astype(jnp.bfloat16)
+
+    def gradient(columns, residual_rows):
+        return jnp.einsum(
+            "ti,tj->ij", columns, residual_rows, preferred_element_type=jnp.float32
+        ).astype(jnp.bfloat16)
 
     if pair:
         me = lax.axis_index("fsdp")
         own = lax.dynamic_slice_in_dim(normed, me * rows, rows, 1)
         far = lax.dynamic_slice_in_dim(normed, (1 - me) * rows, rows, 1)
-        projected = product(own, weights) + product(far, other_weights)
+        far_left, right_sent = lax.optimization_barrier((far_left, right))
+        far_right = lax.ppermute(right_sent, "fsdp", swap)
+        rest = residual(product(own, left) + product(far, far_left), targets[0, :, :half])
+        left_sent, own_left = gradient(far, rest), gradient(own, rest)
+        left_grad = lax.ppermute(left_sent, "fsdp", swap)
+        rest = residual(product(own, right) + product(far, far_right), targets[0, :, half:])
+        right_sent, own_left, count, arrived = lax.optimization_barrier(
+            (gradient(far, rest), own_left, count, arrived)
+        )
+        right_grad = lax.ppermute(right_sent, "fsdp", swap)
+        own_grads, far_grads = (own_left, gradient(own, rest)), (left_grad, right_grad)
     else:
-        projected = product(normed, all_weights)
-    projected = projected / math.sqrt(width_in)
-    residual_rows = ((projected - targets[0].astype(jnp.float32)) * mask[:, None]).astype(
-        jnp.bfloat16
-    )
-
-    def gradient(columns):
-        return jnp.einsum(
-            "ti,tj->ij", columns, residual_rows, preferred_element_type=jnp.float32
-        ).astype(jnp.bfloat16)
-
-    if pair:
-        sent_grad, arrived = lax.optimization_barrier((gradient(far), arrived))
-        far_grad = lax.ppermute(sent_grad, "fsdp", swap)
-        own_grad = gradient(own)
-    else:
+        rest = residual(product(normed, all_weights), targets[0])
         own_grad = lax.psum_scatter(
-            gradient(normed), "fsdp", scatter_dimension=0, tiled=True
+            gradient(normed, rest), "fsdp", scatter_dimension=0, tiled=True
         )
-        far_grad = jnp.zeros_like(own_grad)
+        own_grads, far_grads = (own_grad,), (jnp.zeros_like(own_grad),)
 
     new_params, new_momentum, steps = outer_update(
         arrived, module_params, momentum, module_of_path, sharing_counts
     )
     steps = lax.all_to_all(steps, "path", 0, 0, tiled=True)
-    next_weights = finish(weights, own_grad, far_grad, steps, count)[None]
+    next_weights = finish(weights, own_grads, far_grads, steps, count)[None]
     return (next_weights, new_params, new_momentum)
 
 

time: 266 us -> 244 us (0.917)
  waiting for transfers between devices: 176 us -> 160 us
  Pallas kernels: 29.7 us -> 19.9 us
  matrix products: 22 us -> 30.3 us
  local copies, waits for them, and re-layouts: 15.8 us -> 10.9 us
    ppermute x1, waiting for transfers between devices: 90.4 us -> 0.01 us  [per_device(): count = (counted + lax.ppermute(counted, 'fsdp', swap))[0, 0]]
    ppermute x2 -> x4, waiting for transfers between devices: 85.4 us -> 160 us  [the longest x1 44.4 us: per_device(): right_grad = lax.ppermute(right_sent, 'fsdp', swap)]
    pallas_call x2, Pallas kernels: 22.4 us -> 11.8 us  [the longest x1 8.57 us: finish(): pl.pallas_call(kernel, grid=(parts * turns,), in_specs=[pl.BlockSpec((1,...]
    unnamed x32 -> x36, local copies, waits for them, and re-layouts: 14.7 us -> 4.81 us
    dot_general x2 -> x4, matrix products: 9.87 us -> 16 us  [product(): return jnp.dot(a, b, preferred_element_type=jnp.float32)]
    slice x0 -> x1, local copies, waits for them, and re-layouts: none -> 4.83 us  [per_device(): left, right = (weights[:, :half], weights[:, half:])]
    dot_general x2 -> x4, matrix products: 12.1 us -> 14.4 us  [gradient(): jnp.einsum('ti,tj->ij', columns, residual_rows, preferred_element_type=jn...]
  transfers between devices with their start and end apart: 5 -> 7, of which waited for: 2 -> 4; matrix products, arithmetic and copies ran while one was open for 10% -> 16% of each run, Pallas kernels for 0% -> 0%
where the time goes in v3:
time: 244 us
  waiting for transfers between devices  160 us (66%)
  matrix products  30.3 us (12%)
  Pallas kernels  19.9 us (8%)
  starting transfers between devices  18.9 us (8%)
  local copies, waits for them, and re-layouts  10.9 us (4%)
  other arithmetic  2.57 us (1%)
    ppermute x1, waiting for transfers between devices, per_device(): right_grad = lax.ppermute(right_sent, 'fsdp', swap)  44.4 us
    ppermute x1, waiting for transfers between devices, per_device(): far_left = lax.ppermute(left, 'fsdp', swap)  43.5 us
    ppermute x1, waiting for transfers between devices, per_device(): left_grad = lax.ppermute(left_sent, 'fsdp', swap)  42.9 us
    ppermute x1, waiting for transfers between devices, per_device(): far_right = lax.ppermute(right_sent, 'fsdp', swap)  28.9 us
    dot_general x4, matrix products, product(): return jnp.dot(a, b, preferred_element_type=jnp.float32)  16 us
    dot_general x4, matrix products, gradient(): jnp.einsum('ti,tj->ij', columns, residual_rows, preferred_element_type=jn...  14.4 us
    pallas_call x1, Pallas kernels, finish(): pl.pallas_call(kernel, grid=(parts * turns,), in_specs=[pl.BlockSpec((1,...  8.57 us
    pallas_call x1, Pallas kernels, outer_update(): pl.pallas_call(kernel, grid=(rows // tile,), in_specs=[table, table, bloc...  8.12 us
  transfers between devices with their start and end apart: 7, of which 4 were waited for; matrix products, arithmetic and copies ran while one was open for 16% of the time, Pallas kernels for 0%

profile of v3, /device:TPU:0, one launch (start us, length us, event | category | flops | bytes accessed | tf_op | source)
XLA Modules:
  0.0 243.8 jit_solution(17948748600726311036)
XLA Ops:
  0.6 3.2 %shard_map.112 = bf16[16,1024,128]{2,1,0:T(8,128)(2,1)S(1)} custom-call(bf16[1024,2048]{1,0:T(8,128)(2,1)} %bitcast.24), custom_call_target="tpu_custom_call" | custom-call | bytes 8388608 | tf_op jit(solution)/shard_map/pallas_call | solution.py:28
  3.9 2.0 copy-done
  5.9 7.4 %all-to-all-start = ((bf16[16,1024,128]{2,1,0:T(8,128)(2,1)}), bf16[16,1024,128]{2,1,0:T(8,128)(2,1)}, u32[]{:S(2)}, u32[]{:S(2)}) async-start(bf16[16,1024,128]{2,1,0:T(8,128)(2,1)} %copy-done), calls=%async_computation | async-start | bytes 8388608 | tf_op jit(solution)/shard_map/all_to_all | solution.py:164
  13.4 4.8 %fusion.28 = (bf16[1024,1024]{1,0:T(8,128)(2,1)}, bf16[1024,1024]{1,0:T(8,128)(2,1)}) fusion(bf16[1024,2048]{1,0:T(8,128)(2,1)} %bitcast.20), kind=kLoop, calls=%fused_computation.39 | loop fusion | bytes 8388608 | tf_op jit(solution)/shard_map/slice | solution.py:158
  18.2 1.5 collective-permute-start
  19.7 0.7 fusion.16
  20.4 0.6 broadcast_in_dim.12
  21.0 0.6 collective-permute-start.2
  21.6 0.7 fusion
  22.3 0.6 fusion.1
  22.9 43.5 %collective-permute-done = bf16[1024,1024]{1,0:T(8,128)(2,1)} collective-permute-done((bf16[1024,1024]{1,0:T(8,128)(2,1)}, bf16[1024,1024]{1,0:T(8,128)(2,1)}, u32[]{:S(2)}, u32[]{:S(2)}) %collective-permute-start) | collective-permute-done | bytes 2097184 | tf_op jit(solution)/shard_map/ppermute | solution.py:159
  66.4 1.5 collective-permute-start.1
  67.9 3.5 %fusion.8 = f32[768,1024]{1,0:T(8,128)} fusion(bf16[768,2048]{1,0:T(8,128)(2,1)S(1)} %fusion.1, s32[]{:T(128)S(6)} %select_n.7, bf16[1024,2048]{1,0:T(8,128)(2,1)S(1)} %bitcast.22), kind=kOutput, calls=%fused_computation.16 | convolution fusion | flops 1610612736 | bytes 6815748 | tf_op jit(solution)/shard_map/dot_general | solution.py:171
  71.4 3.4 %fusion.10 = f32[768,1024]{1,0:T(8,128)} fusion(bf16[768,2048]{1,0:T(8,128)(2,1)S(1)} %fusion.1, s32[]{:T(128)S(6)} %select_n.7, bf16[1024,2048]{1,0:T(8,128)(2,1)S(1)} %bitcast.23), kind=kOutput, calls=%fused_computation.18 | convolution fusion | flops 1610612736 | bytes 6815748 | tf_op jit(solution)/shard_map/dot_general | solution.py:171
  74.8 0.6 broadcast_add_fusion
  75.5 0.6 slice.19
  76.1 5.5 %fusion.3 = bf16[768,1024]{1,0:T(8,128)(2,1)S(1)} fusion(f32[768,1024]{1,0:T(8,128)} %fusion.8, bf16[1024,1024]{1,0:T(8,128)(2,1)} %collective-permute-done, bf16[1,768,2048]{2,1,0:T(8,128)(2,1)} %param.10, f32[768]{0:T(1024)S(1)} %get-tuple-element.22, bf16[768,2048]{1,0:T(8,128)(2,1)} %copy-done.8, s32[]{:T(128)S(6)} %select_n.6), kind=kOutput, calls=%fused_computation.6 | convolution fusion | flops 1615331328 | bytes 9964548 | tf_op jit(solution)/shard_map/dot_general | solution.py:171
  81.6 3.3 %convolution_convert_fusion.2.refs_0_ = bf16[1024,1024]{1,0:T(8,128)(2,1)} fusion(bf16[768,1024]{1,0:T(8,128)(2,1)S(1)} %fusion.3, bf16[768,2048]{1,0:T(8,128)(2,1)S(1)} %copy-done.9, s32[]{:T(128)S(6)} %select_n.7), kind=kOutput, calls=%fused_computation.12 | convolution fusion | flops 1611661312 | bytes 5242884 | tf_op jit(solution)/shard_map/ti,tj->ij/dot_general | solution.py:178
  84.9 28.9 %collective-permute-done.1 = bf16[1024,1024]{1,0:T(8,128)(2,1)} collective-permute-done((bf16[1024,1024]{1,0:T(8,128)(2,1)}, bf16[1024,1024]{1,0:T(8,128)(2,1)}, u32[]{:S(2)}, u32[]{:S(2)}) %collective-permute-start.1) | collective-permute-done | bytes 2097184 | tf_op jit(solution)/shard_map/ppermute | solution.py:187
  113.8 3.6 %fusion.5 = bf16[768,1024]{1,0:T(8,128)(2,1)S(1)} fusion(f32[768,1024]{1,0:T(8,128)S(1)} %copy-done.14, bf16[1024,1024]{1,0:T(8,128)(2,1)} %collective-permute-done.1, f32[768]{0:T(1024)S(1)} %get-tuple-element.22, bf16[1,768,2048]{2,1,0:T(8,128)(2,1)S(1)} %copy-done.13, bf16[768,2048]{1,0:T(8,128)(2,1)S(1)} %copy-done.9, s32[]{:T(128)S(6)} %select_n.6), kind=kOutput, calls=%fused_computation.9 | convolution fusion | flops 1615331328 | bytes 9965572 | tf_op jit(solution)/shard_map/dot_general | solution.py:171
  117.4 1.1 copy-done.15
  118.6 3.2 %convolution_convert_fusion.3 = bf16[1024,1024]{1,0:T(8,128)(2,1)} fusion(bf16[768,1024]{1,0:T(8,128)(2,1)S(1)} %fusion.5, bf16[768,2048]{1,0:T(8,128)(2,1)S(1)} %copy-done.9, s32[]{:T(128)S(6)} %select_n.6), kind=kOutput, calls=%fused_computation.13 | convolution fusion | flops 1611661312 | bytes 5242884 | tf_op jit(solution)/shard_map/ti,tj->ij/dot_general | solution.py:178
  121.8 1.6 copy-done.2
  123.4 8.1 %shard_map.113 = (f32[4,1024,128]{2,1,0:T(8,128)}, f32[4,1024,128]{2,1,0:T(8,128)}, bf16[16,1024,128]{2,1,0:T(8,128)(2,1)}) custom-call(s32[16]{0:T(128)S(1)} %copy-done.4, s32[4]{0:T(128)S(1)} %copy-done.5, bf16[16,1024,128]{2,1,0:T(8,128)(2,1)} %all-to-all-done.arrived_ref, f32[4,1024,128]{2,1,0:T(8,128)S(1)} %copy-done.1, f32[4,1024,128]{2,1,0:T(8,128)S(1)} %copy-done.2), custom_call_target="tpu_custom_call" | custom-call | flops 8388608 | bytes 16777216 | tf_op jit(solution)/shard_map/pallas_call | solution.py:68
  131.5 5.8 %all-to-all-start.1 = ((bf16[16,1024,128]{2,1,0:T(8,128)(2,1)}), bf16[16,1024,128]{2,1,0:T(8,128)(2,1)}, u32[]{:S(2)}, u32[]{:S(2)}) async-start(bf16[16,1024,128]{2,1,0:T(8,128)(2,1)} %get-tuple-element.16), calls=%async_computation.1 | async-start | bytes 8388608 | tf_op jit(solution)/shard_map/all_to_all | solution.py:207
  137.4 4.7 %convolution_convert_fusion.1 = bf16[1024,1024]{1,0:T(8,128)(2,1)} fusion(bf16[768,1024]{1,0:T(8,128)(2,1)} %copy-done.17, bf16[768,2048]{1,0:T(8,128)(2,1)S(1)} %copy-done.10, s32[]{:T(128)S(6)} %select_n.6), kind=kOutput, calls=%fused_computation.11 | convolution fusion | flops 1611661312 | bytes 5242884 | tf_op jit(solution)/shard_map/ti,tj->ij/dot_general | solution.py:178
  142.1 1.5 collective-permute-start.3
  143.6 0.5 collective-permute-start.4
  144.1 3.2 %convolution_convert_fusion.refs_2_ = bf16[1024,1024]{1,0:T(8,128)(2,1)} fusion(bf16[768,1024]{1,0:T(8,128)(2,1)S(1)} %copy-done.16, bf16[768,2048]{1,0:T(8,128)(2,1)S(1)} %copy-done.11, s32[]{:T(128)S(6)} %select_n.7), kind=kOutput, calls=%fused_computation.10 | convolution fusion | flops 1611661312 | bytes 5242884 | tf_op jit(solution)/shard_map/ti,tj->ij/dot_general | solution.py:178
  148.0 42.9 %collective-permute-done.3.refs_1_ = bf16[1024,1024]{1,0:T(8,128)(2,1)} collective-permute-done((bf16[1024,1024]{1,0:T(8,128)(2,1)}, bf16[1024,1024]{1,0:T(8,128)(2,1)}, u32[]{:S(2)}, u32[]{:S(2)}) %collective-permute-start.3) | collective-permute-done | bytes 2097184 | tf_op jit(solution)/shard_map/ppermute | solution.py:190
  190.9 44.4 %collective-permute-done.4.refs_3_ = bf16[1024,1024]{1,0:T(8,128)(2,1)} collective-permute-done((bf16[1024,1024]{1,0:T(8,128)(2,1)}, bf16[1024,1024]{1,0:T(8,128)(2,1)}, u32[]{:S(2)}, u32[]{:S(2)}) %collective-permute-start.4) | collective-permute-done | bytes 2097184 | tf_op jit(solution)/shard_map/ppermute | solution.py:195
  235.3 8.6 %shard_map.114 = bf16[1024,2048]{1,0:T(8,128)(2,1)} custom-call(f32[1,128]{1,0:T(1,128)S(1)} %broadcast_in_dim.13.root_ref, bf16[1024,2048]{1,0:T(8,128)(2,1)} %bitcast.21, bf16[16,1024,128]{2,1,0:T(8,128)(2,1)} %all-to-all-done.1.steps_ref, bf16[1024,1024]{1,0:T(8,128)(2,1)S(1)} %copy-done.3, bf16[1024,1024]{1,0:T(8,128)(2,1)} %collective-permute-done.3.refs_1_, ...), custom_call_target="tpu_custom_call" | custom-call | flops 12582912 | bytes 20971520 | tf_op jit(solution)/shard_map/pallas_call | solution.py:118
  (38 shorter events, 0.1 us)
Async XLA Ops:
  3.9 2.0 copy-start
  5.9 115.8 %all-to-all-start = ((bf16[16,1024,128]{2,1,0:T(8,128)(2,1)}), bf16[16,1024,128]{2,1,0:T(8,128)(2,1)}, u32[]{:S(2)}, u32[]{:S(2)}) async-start(bf16[16,1024,128]{2,1,0:T(8,128)(2,1)} %copy-done), calls=%async_computation | async-start | bytes 8388608 | tf_op jit(solution)/shard_map/all_to_all | solution.py:164
  13.3 6.4 %copy-start.12 = (s32[1,768]{1,0:T(1,128)S(1)}, s32[1,768]{1,0:T(1,128)}, u32[]{:S(2)}) copy-start(s32[1,768]{1,0:T(1,128)} %param.11) | copy-start | bytes 9220
  13.3 8.3 %copy-start.7 = (bf16[1,768,2048]{2,1,0:T(8,128)(2,1)S(1)}, bf16[1,768,2048]{2,1,0:T(8,128)(2,1)}, u32[]{:S(2)}) copy-start(bf16[1,768,2048]{2,1,0:T(8,128)(2,1)} %param.9) | copy-start | bytes 9437188
  18.2 48.2 %collective-permute-start = (bf16[1024,1024]{1,0:T(8,128)(2,1)}, bf16[1024,1024]{1,0:T(8,128)(2,1)}, u32[]{:S(2)}, u32[]{:S(2)}) collective-permute-start(bf16[1024,1024]{1,0:T(8,128)(2,1)} %get-tuple-element.24), channel_id=1, source_target_pairs={{0,1},{1,0},{2,3},{3,2},{4,5},{5,4},{6,7},{7,6},{8,9},{9,8},{10,11... | collective-permute-start | bytes 6291464 | tf_op jit(solution)/shard_map/ppermute | solution.py:159
  21.0 53.8 %collective-permute-start.2 = (f32[8,128]{1,0:T(8,128)S(1)}, f32[8,128]{1,0:T(8,128)S(1)}, u32[]{:S(2)}, u32[]{:S(2)}) collective-permute-start(f32[8,128]{1,0:T(8,128)S(1)} %broadcast_in_dim.12), channel_id=1, source_target_pairs={{0,1},{1,0},{2,3},{3,2},{4,5},{5,4},{6,7},{7,6},{8,9},{9,8},{10,11... | collective-permute-start | bytes 12296 | tf_op jit(solution)/shard_map/ppermute | solution.py:156
  22.3 45.6 %copy-start.6 = (bf16[1,1024,2048]{2,1,0:T(8,128)(2,1)S(1)}, bf16[1,1024,2048]{2,1,0:T(8,128)(2,1)}, u32[]{:S(2)}) copy-start(bf16[1,1024,2048]{2,1,0:T(8,128)(2,1)} %param.12) | copy-start | bytes 12582916
  22.9 48.5 %copy-start.8 = (bf16[768,2048]{1,0:T(8,128)(2,1)}, bf16[768,2048]{1,0:T(8,128)(2,1)S(1)}, u32[]{:S(2)}) copy-start(bf16[768,2048]{1,0:T(8,128)(2,1)S(1)} %fusion.1) | copy-start | bytes 9437188
  66.4 47.4 %collective-permute-start.1 = (bf16[1024,1024]{1,0:T(8,128)(2,1)}, bf16[1024,1024]{1,0:T(8,128)(2,1)}, u32[]{:S(2)}, u32[]{:S(2)}) collective-permute-start(bf16[1024,1024]{1,0:T(8,128)(2,1)} %get-tuple-element.12), channel_id=1, source_target_pairs={{0,1},{1,0},{2,3},{3,2},{4,5},{5,4},{6,7},{7,6},{8,9},{9,8},{10,11... | collective-permute-start | bytes 6291464 | tf_op jit(solution)/shard_map/ppermute | solution.py:187
  76.1 5.5 %copy-start.9 = (bf16[768,2048]{1,0:T(8,128)(2,1)S(1)}, bf16[768,2048]{1,0:T(8,128)(2,1)}, u32[]{:S(2)}) copy-start(bf16[768,2048]{1,0:T(8,128)(2,1)} %copy-done.8) | copy-start | bytes 9437188
  81.6 3.3 %copy-start.17 = (bf16[768,1024]{1,0:T(8,128)(2,1)}, bf16[768,1024]{1,0:T(8,128)(2,1)S(1)}, u32[]{:S(2)}) copy-start(bf16[768,1024]{1,0:T(8,128)(2,1)S(1)} %fusion.3) | copy-start | bytes 4718596
  81.6 32.2 %copy-start.13 = (bf16[1,768,2048]{2,1,0:T(8,128)(2,1)S(1)}, bf16[1,768,2048]{2,1,0:T(8,128)(2,1)}, u32[]{:S(2)}) copy-start(bf16[1,768,2048]{2,1,0:T(8,128)(2,1)} %param.10) | copy-start | bytes 9437188
  81.6 32.2 %copy-start.14 = (f32[768,1024]{1,0:T(8,128)S(1)}, f32[768,1024]{1,0:T(8,128)}, u32[]{:S(2)}) copy-start(f32[768,1024]{1,0:T(8,128)} %fusion.10) | copy-start | bytes 9437188
  117.4 1.2 copy-start.15
  118.6 3.2 %copy-start.1 = (f32[4,1024,128]{2,1,0:T(8,128)S(1)}, f32[4,1024,128]{2,1,0:T(8,128)}, u32[]{:S(2)}) copy-start(f32[4,1024,128]{2,1,0:T(8,128)} %params_ref.1) | copy-start | bytes 6291460
  118.6 3.2 %copy-start.4 = (s32[16]{0:T(128)S(1)}, s32[16]{0:T(128)}, u32[]{:S(2)}) copy-start(s32[16]{0:T(128)} %module_ref.1) | copy-start | bytes 196
  118.6 3.2 %copy-start.5 = (s32[4]{0:T(128)S(1)}, s32[4]{0:T(128)}, u32[]{:S(2)}) copy-start(s32[4]{0:T(128)} %count_ref.1) | copy-start | bytes 52
  121.8 1.6 copy-start.2
  131.5 5.9 %copy-start.10 = (bf16[768,2048]{1,0:T(8,128)(2,1)S(1)}, bf16[768,2048]{1,0:T(8,128)(2,1)}, u32[]{:S(2)}) copy-start(bf16[768,2048]{1,0:T(8,128)(2,1)} %copy-done.8) | copy-start | bytes 9437188
  131.5 103.8 %all-to-all-start.1 = ((bf16[16,1024,128]{2,1,0:T(8,128)(2,1)}), bf16[16,1024,128]{2,1,0:T(8,128)(2,1)}, u32[]{:S(2)}, u32[]{:S(2)}) async-start(bf16[16,1024,128]{2,1,0:T(8,128)(2,1)} %get-tuple-element.16), calls=%async_computation.1 | async-start | bytes 8388608 | tf_op jit(solution)/shard_map/all_to_all | solution.py:207
  137.3 6.8 %copy-start.11 = (bf16[768,2048]{1,0:T(8,128)(2,1)S(1)}, bf16[768,2048]{1,0:T(8,128)(2,1)}, u32[]{:S(2)}) copy-start(bf16[768,2048]{1,0:T(8,128)(2,1)} %copy-done.8) | copy-start | bytes 9437188
  137.3 6.8 %copy-start.16 = (bf16[768,1024]{1,0:T(8,128)(2,1)S(1)}, bf16[768,1024]{1,0:T(8,128)(2,1)}, u32[]{:S(2)}) copy-start(bf16[768,1024]{1,0:T(8,128)(2,1)} %copy-done.15) | copy-start | bytes 4718596
  142.1 93.1 %copy-start.3 = (bf16[1024,1024]{1,0:T(8,128)(2,1)S(1)}, bf16[1024,1024]{1,0:T(8,128)(2,1)}, u32[]{:S(2)}) copy-start(bf16[1024,1024]{1,0:T(8,128)(2,1)} %convolution_convert_fusion.2.refs_0_) | copy-start | bytes 6291460
  142.1 48.8 %collective-permute-start.3 = (bf16[1024,1024]{1,0:T(8,128)(2,1)}, bf16[1024,1024]{1,0:T(8,128)(2,1)}, u32[]{:S(2)}, u32[]{:S(2)}) collective-permute-start(bf16[1024,1024]{1,0:T(8,128)(2,1)} %convolution_convert_fusion.1), channel_id=1, source_target_pairs={{0,1},{1,0},{2,3},{3,2},{4,5},{5,4},{6,7},{7,6},{8,9},{9,8},{10,11... | collective-permute-start | bytes 6291464 | tf_op jit(solution)/shard_map/ppermute | solution.py:190
  143.6 91.6 %collective-permute-start.4 = (bf16[1024,1024]{1,0:T(8,128)(2,1)}, bf16[1024,1024]{1,0:T(8,128)(2,1)}, u32[]{:S(2)}, u32[]{:S(2)}) collective-permute-start(bf16[1024,1024]{1,0:T(8,128)(2,1)} %convolution_convert_fusion.3), channel_id=1, source_target_pairs={{0,1},{1,0},{2,3},{3,2},{4,5},{5,4},{6,7},{7,6},{8,9},{9,8},{10,11... | collective-permute-start | bytes 6291464 | tf_op jit(solution)/shard_map/ppermute | solution.py:195

commit v4 on v3

--- a/solution.py
+++ b/solution.py
@@ -187,7 +187,8 @@
         far_right = lax.ppermute(right_sent, "fsdp", swap)
         rest = residual(product(own, left) + product(far, far_left), targets[0, :, :half])
         left_sent, own_left = gradient(far, rest), gradient(own, rest)
-        left_grad = lax.ppermute(left_sent, "fsdp", swap)
+        far_right, left_ready = lax.optimization_barrier((far_right, left_sent))
+        left_grad = lax.ppermute(left_ready, "fsdp", swap)
         rest = residual(product(own, right) + product(far, far_right), targets[0, :, half:])
         right_sent, own_left, count, arrived = lax.optimization_barrier(
             (gradient(far, rest), own_left, count, arrived)

time: 244 us -> 240 us (0.984)
  waiting for transfers between devices: 160 us -> 156 us
    ppermute x1, waiting for transfers between devices: 28.9 us -> 26.4 us  [per_device(): far_right = lax.ppermute(right_sent, 'fsdp', swap)]
where the time goes in v4:
time: 240 us; the launch traced here: 239 us
  waiting for transfers between devices  156 us (65%)
  matrix products  30.4 us (13%)
  Pallas kernels  19.9 us (8%)
  starting transfers between devices  18.7 us (8%)
  local copies, waits for them, and re-layouts  10.7 us (4%)
    ppermute x1, waiting for transfers between devices, per_device(): right_grad = lax.ppermute(right_sent, 'fsdp', swap)  44.4 us
    ppermute x1, waiting for transfers between devices, per_device(): far_left = lax.ppermute(left, 'fsdp', swap)  43.7 us
    ppermute x1, waiting for transfers between devices, per_device(): left_grad = lax.ppermute(left_ready, 'fsdp', swap)  41.1 us
    ppermute x1, waiting for transfers between devices, per_device(): far_right = lax.ppermute(right_sent, 'fsdp', swap)  26.4 us
    dot_general x4, matrix products, product(): return jnp.dot(a, b, preferred_element_type=jnp.float32)  15.5 us
    dot_general x4, matrix products, gradient(): jnp.einsum('ti,tj->ij', columns, residual_rows, preferred_element_type=jn...  14.8 us
    pallas_call x1, Pallas kernels, finish(): pl.pallas_call(kernel, grid=(parts * turns,), in_specs=[pl.BlockSpec((1,...  8.57 us
    pallas_call x1, Pallas kernels, outer_update(): pl.pallas_call(kernel, grid=(rows // tile,), in_specs=[table, table, bloc...  8.11 us
  transfers between devices with their start and end apart: 7, of which 4 were waited for; matrix products, arithmetic and copies ran while one was open for 16% of the time, Pallas kernels for 0%

profile of v4, /device:TPU:0, one launch (start us, length us, event | category | flops | bytes accessed | tf_op | source)
XLA Modules:
  0.0 239.1 jit_solution(12886578733034422337)
XLA Ops:
  0.6 3.2 %shard_map.112 = bf16[16,1024,128]{2,1,0:T(8,128)(2,1)S(1)} custom-call(bf16[1024,2048]{1,0:T(8,128)(2,1)} %bitcast.24), custom_call_target="tpu_custom_call" | custom-call | bytes 8388608 | tf_op jit(solution)/shard_map/pallas_call | solution.py:28
  3.9 2.0 copy-done
  5.9 7.4 %all-to-all-start = ((bf16[16,1024,128]{2,1,0:T(8,128)(2,1)}), bf16[16,1024,128]{2,1,0:T(8,128)(2,1)}, u32[]{:S(2)}, u32[]{:S(2)}) async-start(bf16[16,1024,128]{2,1,0:T(8,128)(2,1)} %copy-done), calls=%async_computation | async-start | bytes 8388608 | tf_op jit(solution)/shard_map/all_to_all | solution.py:164
  13.4 4.8 %fusion.28 = (bf16[1024,1024]{1,0:T(8,128)(2,1)}, bf16[1024,1024]{1,0:T(8,128)(2,1)}) fusion(bf16[1024,2048]{1,0:T(8,128)(2,1)} %bitcast.20), kind=kLoop, calls=%fused_computation.39 | loop fusion | bytes 8388608 | tf_op jit(solution)/shard_map/slice | solution.py:158
  18.2 1.5 collective-permute-start
  19.7 0.6 fusion.16
  20.3 0.5 broadcast_in_dim.12
  20.8 0.6 collective-permute-start.2
  21.4 0.7 fusion
  22.1 0.6 fusion.1
  22.7 43.7 %collective-permute-done = bf16[1024,1024]{1,0:T(8,128)(2,1)} collective-permute-done((bf16[1024,1024]{1,0:T(8,128)(2,1)}, bf16[1024,1024]{1,0:T(8,128)(2,1)}, u32[]{:S(2)}, u32[]{:S(2)}) %collective-permute-start) | collective-permute-done | bytes 2097184 | tf_op jit(solution)/shard_map/ppermute | solution.py:159
  66.4 1.5 collective-permute-start.1
  67.9 3.4 %fusion.8 = f32[768,1024]{1,0:T(8,128)} fusion(bf16[768,2048]{1,0:T(8,128)(2,1)S(1)} %fusion.1, s32[]{:T(128)S(6)} %select_n.7, bf16[1024,2048]{1,0:T(8,128)(2,1)S(1)} %bitcast.22), kind=kOutput, calls=%fused_computation.16 | convolution fusion | flops 1610612736 | bytes 6815748 | tf_op jit(solution)/shard_map/dot_general | solution.py:171
  71.4 3.4 %fusion.10 = f32[768,1024]{1,0:T(8,128)} fusion(bf16[768,2048]{1,0:T(8,128)(2,1)S(1)} %fusion.1, s32[]{:T(128)S(6)} %select_n.7, bf16[1024,2048]{1,0:T(8,128)(2,1)S(1)} %bitcast.23), kind=kOutput, calls=%fused_computation.18 | convolution fusion | flops 1610612736 | bytes 6815748 | tf_op jit(solution)/shard_map/dot_general | solution.py:171
  74.8 0.5 broadcast_add_fusion
  75.4 0.5 slice.19
  75.8 5.1 %fusion.5 = bf16[768,1024]{1,0:T(8,128)(2,1)S(1)} fusion(f32[768,1024]{1,0:T(8,128)} %fusion.8, bf16[1024,1024]{1,0:T(8,128)(2,1)} %collective-permute-done, f32[768]{0:T(1024)S(1)} %get-tuple-element.26, bf16[1,768,2048]{2,1,0:T(8,128)(2,1)S(1)} %copy-done.11, bf16[768,2048]{1,0:T(8,128)(2,1)} %copy-done.8, s32[]{:T(128)S(6)} %select_n.6), kind=kOutput, calls=%fused_computation.9 | convolution fusion | flops 1615331328 | bytes 9964548 | tf_op jit(solution)/shard_map/dot_general | solution.py:171
  81.0 3.3 %convolution_convert_fusion.1.refs_0_ = bf16[1024,1024]{1,0:T(8,128)(2,1)} fusion(bf16[768,1024]{1,0:T(8,128)(2,1)S(1)} %fusion.5, bf16[768,2048]{1,0:T(8,128)(2,1)S(1)} %copy-done.9, s32[]{:T(128)S(6)} %select_n.7), kind=kOutput, calls=%fused_computation.11 | convolution fusion | flops 1611661312 | bytes 5242884 | tf_op jit(solution)/shard_map/ti,tj->ij/dot_general | solution.py:178
  84.2 3.2 %convolution_convert_fusion.3 = bf16[1024,1024]{1,0:T(8,128)(2,1)} fusion(bf16[768,1024]{1,0:T(8,128)(2,1)S(1)} %fusion.5, bf16[768,2048]{1,0:T(8,128)(2,1)S(1)} %copy-done.9, s32[]{:T(128)S(6)} %select_n.6), kind=kOutput, calls=%fused_computation.13 | convolution fusion | flops 1611661312 | bytes 5242884 | tf_op jit(solution)/shard_map/ti,tj->ij/dot_general | solution.py:178
  87.4 26.4 %collective-permute-done.1 = bf16[1024,1024]{1,0:T(8,128)(2,1)} collective-permute-done((bf16[1024,1024]{1,0:T(8,128)(2,1)}, bf16[1024,1024]{1,0:T(8,128)(2,1)}, u32[]{:S(2)}, u32[]{:S(2)}) %collective-permute-start.1) | collective-permute-done | bytes 2097184 | tf_op jit(solution)/shard_map/ppermute | solution.py:187
  113.8 3.6 %fusion.3 = bf16[768,1024]{1,0:T(8,128)(2,1)S(1)} fusion(f32[768,1024]{1,0:T(8,128)S(1)} %copy-done.12, bf16[1024,1024]{1,0:T(8,128)(2,1)} %collective-permute-done.1, bf16[1,768,2048]{2,1,0:T(8,128)(2,1)S(1)} %copy-done.11, f32[768]{0:T(1024)S(1)} %get-tuple-element.26, bf16[768,2048]{1,0:T(8,128)(2,1)S(1)} %copy-done.9, s32[]{:T(128)S(6)} %select_n.6), kind=kOutput, calls=%fused_computation.6 | convolution fusion | flops 1615331328 | bytes 9965572 | tf_op jit(solution)/shard_map/dot_general | solution.py:171
  117.4 1.2 copy-done.13
  118.6 3.4 %convolution_convert_fusion.2 = bf16[1024,1024]{1,0:T(8,128)(2,1)} fusion(bf16[768,1024]{1,0:T(8,128)(2,1)S(1)} %fusion.3, bf16[768,2048]{1,0:T(8,128)(2,1)S(1)} %copy-done.9, s32[]{:T(128)S(6)} %select_n.6), kind=kOutput, calls=%fused_computation.12 | convolution fusion | flops 1611661312 | bytes 5242884 | tf_op jit(solution)/shard_map/ti,tj->ij/dot_general | solution.py:178
  122.0 1.6 copy-done.2
  123.6 8.1 %shard_map.113 = (f32[4,1024,128]{2,1,0:T(8,128)}, f32[4,1024,128]{2,1,0:T(8,128)}, bf16[16,1024,128]{2,1,0:T(8,128)(2,1)}) custom-call(s32[16]{0:T(128)S(1)} %copy-done.4, s32[4]{0:T(128)S(1)} %copy-done.5, bf16[16,1024,128]{2,1,0:T(8,128)(2,1)} %all-to-all-done.arrived_ref, f32[4,1024,128]{2,1,0:T(8,128)S(1)} %copy-done.1, f32[4,1024,128]{2,1,0:T(8,128)S(1)} %copy-done.2), custom_call_target="tpu_custom_call" | custom-call | flops 8388608 | bytes 16777216 | tf_op jit(solution)/shard_map/pallas_call | solution.py:68
  131.7 5.6 %all-to-all-start.1 = ((bf16[16,1024,128]{2,1,0:T(8,128)(2,1)}), bf16[16,1024,128]{2,1,0:T(8,128)(2,1)}, u32[]{:S(2)}, u32[]{:S(2)}) async-start(bf16[16,1024,128]{2,1,0:T(8,128)(2,1)} %get-tuple-element.19), calls=%async_computation.1 | async-start | bytes 8388608 | tf_op jit(solution)/shard_map/all_to_all | solution.py:208
  137.3 1.6 collective-permute-start.3
  138.8 0.5 collective-permute-start.4
  139.4 5.0 %convolution_convert_fusion.refs_2_ = bf16[1024,1024]{1,0:T(8,128)(2,1)} fusion(bf16[768,1024]{1,0:T(8,128)(2,1)} %copy-done.13, bf16[768,2048]{1,0:T(8,128)(2,1)} %copy-done.8, s32[]{:T(128)S(6)} %select_n.7), kind=kOutput, calls=%fused_computation.10 | convolution fusion | flops 1611661312 | bytes 5242884 | tf_op jit(solution)/shard_map/ti,tj->ij/dot_general | solution.py:178
  145.0 41.1 %collective-permute-done.3.refs_1_ = bf16[1024,1024]{1,0:T(8,128)(2,1)} collective-permute-done((bf16[1024,1024]{1,0:T(8,128)(2,1)}, bf16[1024,1024]{1,0:T(8,128)(2,1)}, u32[]{:S(2)}, u32[]{:S(2)}) %collective-permute-start.3) | collective-permute-done | bytes 2097184 | tf_op jit(solution)/shard_map/ppermute | solution.py:191
  186.1 44.4 %collective-permute-done.4.refs_3_ = bf16[1024,1024]{1,0:T(8,128)(2,1)} collective-permute-done((bf16[1024,1024]{1,0:T(8,128)(2,1)}, bf16[1024,1024]{1,0:T(8,128)(2,1)}, u32[]{:S(2)}, u32[]{:S(2)}) %collective-permute-start.4) | collective-permute-done | bytes 2097184 | tf_op jit(solution)/shard_map/ppermute | solution.py:196
  230.5 8.6 %shard_map.114 = bf16[1024,2048]{1,0:T(8,128)(2,1)} custom-call(f32[1,128]{1,0:T(1,128)S(1)} %broadcast_in_dim.13.root_ref, bf16[1024,2048]{1,0:T(8,128)(2,1)} %bitcast.21, bf16[16,1024,128]{2,1,0:T(8,128)(2,1)} %all-to-all-done.1.steps_ref, bf16[1024,1024]{1,0:T(8,128)(2,1)S(1)} %copy-done.3, bf16[1024,1024]{1,0:T(8,128)(2,1)} %collective-permute-done.3.refs_1_, ...), custom_call_target="tpu_custom_call" | custom-call | flops 12582912 | bytes 20971520 | tf_op jit(solution)/shard_map/pallas_call | solution.py:118
  (30 shorter events, 0.1 us)
Async XLA Ops:
  3.9 2.0 copy-start
  5.9 116.1 %all-to-all-start = ((bf16[16,1024,128]{2,1,0:T(8,128)(2,1)}), bf16[16,1024,128]{2,1,0:T(8,128)(2,1)}, u32[]{:S(2)}, u32[]{:S(2)}) async-start(bf16[16,1024,128]{2,1,0:T(8,128)(2,1)} %copy-done), calls=%async_computation | async-start | bytes 8388608 | tf_op jit(solution)/shard_map/all_to_all | solution.py:164
  13.3 6.4 %copy-start.10 = (s32[1,768]{1,0:T(1,128)S(1)}, s32[1,768]{1,0:T(1,128)}, u32[]{:S(2)}) copy-start(s32[1,768]{1,0:T(1,128)} %param.11) | copy-start | bytes 9220
  13.3 8.1 %copy-start.7 = (bf16[1,768,2048]{2,1,0:T(8,128)(2,1)S(1)}, bf16[1,768,2048]{2,1,0:T(8,128)(2,1)}, u32[]{:S(2)}) copy-start(bf16[1,768,2048]{2,1,0:T(8,128)(2,1)} %param.9) | copy-start | bytes 9437188
  18.2 48.2 %collective-permute-start = (bf16[1024,1024]{1,0:T(8,128)(2,1)}, bf16[1024,1024]{1,0:T(8,128)(2,1)}, u32[]{:S(2)}, u32[]{:S(2)}) collective-permute-start(bf16[1024,1024]{1,0:T(8,128)(2,1)} %get-tuple-element.28), channel_id=1, source_target_pairs={{0,1},{1,0},{2,3},{3,2},{4,5},{5,4},{6,7},{7,6},{8,9},{9,8},{10,11... | collective-permute-start | bytes 6291464 | tf_op jit(solution)/shard_map/ppermute | solution.py:159
  20.8 54.0 %collective-permute-start.2 = (f32[8,128]{1,0:T(8,128)S(1)}, f32[8,128]{1,0:T(8,128)S(1)}, u32[]{:S(2)}, u32[]{:S(2)}) collective-permute-start(f32[8,128]{1,0:T(8,128)S(1)} %broadcast_in_dim.12), channel_id=1, source_target_pairs={{0,1},{1,0},{2,3},{3,2},{4,5},{5,4},{6,7},{7,6},{8,9},{9,8},{10,11... | collective-permute-start | bytes 12296 | tf_op jit(solution)/shard_map/ppermute | solution.py:156
  22.1 45.8 %copy-start.6 = (bf16[1,1024,2048]{2,1,0:T(8,128)(2,1)S(1)}, bf16[1,1024,2048]{2,1,0:T(8,128)(2,1)}, u32[]{:S(2)}) copy-start(bf16[1,1024,2048]{2,1,0:T(8,128)(2,1)} %param.12) | copy-start | bytes 12582916
  22.7 48.7 %copy-start.8 = (bf16[768,2048]{1,0:T(8,128)(2,1)}, bf16[768,2048]{1,0:T(8,128)(2,1)S(1)}, u32[]{:S(2)}) copy-start(bf16[768,2048]{1,0:T(8,128)(2,1)S(1)} %fusion.1) | copy-start | bytes 9437188
  66.4 47.4 %collective-permute-start.1 = (bf16[1024,1024]{1,0:T(8,128)(2,1)}, bf16[1024,1024]{1,0:T(8,128)(2,1)}, u32[]{:S(2)}, u32[]{:S(2)}) collective-permute-start(bf16[1024,1024]{1,0:T(8,128)(2,1)} %get-tuple-element.14), channel_id=1, source_target_pairs={{0,1},{1,0},{2,3},{3,2},{4,5},{5,4},{6,7},{7,6},{8,9},{9,8},{10,11... | collective-permute-start | bytes 6291464 | tf_op jit(solution)/shard_map/ppermute | solution.py:187
  71.4 4.5 %copy-start.11 = (bf16[1,768,2048]{2,1,0:T(8,128)(2,1)S(1)}, bf16[1,768,2048]{2,1,0:T(8,128)(2,1)}, u32[]{:S(2)}) copy-start(bf16[1,768,2048]{2,1,0:T(8,128)(2,1)} %param.10) | copy-start | bytes 9437188
  75.8 5.1 %copy-start.9 = (bf16[768,2048]{1,0:T(8,128)(2,1)S(1)}, bf16[768,2048]{1,0:T(8,128)(2,1)}, u32[]{:S(2)}) copy-start(bf16[768,2048]{1,0:T(8,128)(2,1)} %copy-done.8) | copy-start | bytes 9437188
  84.2 29.6 %copy-start.12 = (f32[768,1024]{1,0:T(8,128)S(1)}, f32[768,1024]{1,0:T(8,128)}, u32[]{:S(2)}) copy-start(f32[768,1024]{1,0:T(8,128)} %fusion.10) | copy-start | bytes 9437188
  117.4 1.2 copy-start.13
  118.6 3.4 %copy-start.1 = (f32[4,1024,128]{2,1,0:T(8,128)S(1)}, f32[4,1024,128]{2,1,0:T(8,128)}, u32[]{:S(2)}) copy-start(f32[4,1024,128]{2,1,0:T(8,128)} %params_ref.1) | copy-start | bytes 6291460
  118.6 3.4 %copy-start.4 = (s32[16]{0:T(128)S(1)}, s32[16]{0:T(128)}, u32[]{:S(2)}) copy-start(s32[16]{0:T(128)} %module_ref.1) | copy-start | bytes 196
  118.6 3.4 %copy-start.5 = (s32[4]{0:T(128)S(1)}, s32[4]{0:T(128)}, u32[]{:S(2)}) copy-start(s32[4]{0:T(128)} %count_ref.1) | copy-start | bytes 52
  122.0 1.6 copy-start.2
  131.7 98.8 %all-to-all-start.1 = ((bf16[16,1024,128]{2,1,0:T(8,128)(2,1)}), bf16[16,1024,128]{2,1,0:T(8,128)(2,1)}, u32[]{:S(2)}, u32[]{:S(2)}) async-start(bf16[16,1024,128]{2,1,0:T(8,128)(2,1)} %get-tuple-element.19), calls=%async_computation.1 | async-start | bytes 8388608 | tf_op jit(solution)/shard_map/all_to_all | solution.py:208
  137.3 93.2 %copy-start.3 = (bf16[1024,1024]{1,0:T(8,128)(2,1)S(1)}, bf16[1024,1024]{1,0:T(8,128)(2,1)}, u32[]{:S(2)}) copy-start(bf16[1024,1024]{1,0:T(8,128)(2,1)} %convolution_convert_fusion.1.refs_0_) | copy-start | bytes 6291460
  137.3 48.8 %collective-permute-start.3 = (bf16[1024,1024]{1,0:T(8,128)(2,1)}, bf16[1024,1024]{1,0:T(8,128)(2,1)}, u32[]{:S(2)}, u32[]{:S(2)}) collective-permute-start(bf16[1024,1024]{1,0:T(8,128)(2,1)} %convolution_convert_fusion.3), channel_id=1, source_target_pairs={{0,1},{1,0},{2,3},{3,2},{4,5},{5,4},{6,7},{7,6},{8,9},{9,8},{10,11... | collective-permute-start | bytes 6291464 | tf_op jit(solution)/shard_map/ppermute | solution.py:191
  138.8 91.7 %collective-permute-start.4 = (bf16[1024,1024]{1,0:T(8,128)(2,1)}, bf16[1024,1024]{1,0:T(8,128)(2,1)}, u32[]{:S(2)}, u32[]{:S(2)}) collective-permute-start(bf16[1024,1024]{1,0:T(8,128)(2,1)} %convolution_convert_fusion.2), channel_id=1, source_target_pairs={{0,1},{1,0},{2,3},{3,2},{4,5},{5,4},{6,7},{7,6},{8,9},{9,8},{10,11... | collective-permute-start | bytes 6291464 | tf_op jit(solution)/shard_map/ppermute | solution.py:196
